TPU v7x, 32 devices: a whole 2x2x4 slice. The times are simulated.
32 devices in a mesh: grp: 2 (over x), ctx: 8 (over z, y), head: 2 (over core).
Axes of the slice: x: 2, y: 2, z: 4, core: 2. Of those that a mesh axis runs over, the one named last changes fastest.
Arguments:
- queries: bfloat16 [3072, 16, 128], P(('grp', 'ctx'), 'head'), parts along dimension 0
- key_vecs: bfloat16 [3072, 16, 128], P(('grp', 'ctx'), 'head'), parts along dimension 0
- value_vecs: bfloat16 [3072, 16, 128], P(('grp', 'ctx'), 'head'), parts along dimension 0, may hold values from -6 to 6
- out_grad: bfloat16 [3072, 16, 128], P(('grp', 'ctx'), 'head'), parts along dimension 0, may hold values from -6 to 6
- doc_ids: int32 [3072], P('grp'), parts along dimension 0, may hold values from 0 to 5, never falling along the last dimension, each value on 1 to 960 neighbouring positions
Outputs:
- attn_out: bfloat16 [3072, 16, 128], P(('grp', 'ctx'), 'head'), parts along dimension 0
- query_grad: bfloat16 [3072, 16, 128], P(('grp', 'ctx'), 'head'), parts along dimension 0
- key_grad: bfloat16 [3072, 16, 128], P(('grp', 'ctx'), 'head'), parts along dimension 0
- value_grad: bfloat16 [3072, 16, 128], P(('grp', 'ctx'), 'head'), parts along dimension 0
There are 2 independent parts, one for each index of `grp`. A program takes and returns all parts, laid end to end along the dimension named above; each array names one. Nothing has to cross between parts.
Inputs may be any that keep to these rules, and one draw needn't show every extreme that they name: doc_ids never fall along the sequence; every document has 1 to 960 tokens and one has exactly 960.
All inputs are finite; a program needn't handle non-finite values.
Results may differ from a plain program's by a relative error of at most 0.035.
Values may be sent and summed in bfloat16 or wider, within the bound.
A program may use at most 128 MiB of HBM per device.

v0:
```python
import jax
import jax.numpy as jnp
from jax import lax
from jax.sharding import PartitionSpec as P


def block_length(shard_rows, shard_count):
    factor = 1
    while factor * shard_rows < 512 and shard_count % (factor * 2) == 0:
        factor = factor * 2
    return factor * shard_rows


def stored_position(rows, shard_rows, shard_count):
    half_rows = shard_rows // 2
    shard = rows // shard_rows
    within = rows % shard_rows
    return jnp.where(
        within < half_rows,
        shard * half_rows + within,
        (2 * shard_count - 1 - shard) * half_rows + within - half_rows,
    )


def score_block(query_blk, query_pos, query_doc, key_blk, key_pos, key_doc, scaling):
    scores = (
        jnp.einsum("qhd,khd->hqk", query_blk, key_blk, preferred_element_type=jnp.float32) * scaling
    )
    allowed = (key_doc[None, :] == query_doc[:, None]) & (key_pos[None, :] <= query_pos[:, None])
    return (scores, allowed[None])


def probs_of(scores, allowed, lse):
    return jnp.where(allowed, jnp.exp(scores - lse[:, :, None]), 0.0).astype(jnp.bfloat16)


def dscores_of(probs, grad_blk, value_blk, delta):
    dprobs = jnp.einsum("qhd,khd->hqk", grad_blk, value_blk, preferred_element_type=jnp.float32)
    return (probs.astype(jnp.float32) * (dprobs - delta[:, :, None])).astype(jnp.bfloat16)


def on_device(queries, key_vecs, value_vecs, out_grad, doc_ids):
    shard_rows = queries.shape[0]
    head_count = queries.shape[1]
    head_size = queries.shape[2]
    scaling = head_size ** (-0.5)
    shard_count = lax.axis_size("ctx")
    shard_index = lax.axis_index("ctx")
    own_start = shard_index * shard_rows

    def positions(start, length):
        return stored_position(start + jnp.arange(length, dtype=jnp.int32), shard_rows, shard_count)

    own_pos = positions(own_start, shard_rows)
    own_doc = jnp.take(doc_ids, own_pos)
    keys_all, values_all = (
        lax.all_gather(key_vecs, "ctx", axis=0, tiled=True),
        lax.all_gather(value_vecs, "ctx", axis=0, tiled=True),
    )
    block = block_length(shard_rows, shard_count)
    block_count = keys_all.shape[0] // block

    def key_slices(start, length):
        key_blk = lax.dynamic_slice_in_dim(keys_all, start, length, 0)
        value_blk = lax.dynamic_slice_in_dim(values_all, start, length, 0)
        key_pos = positions(start, length)
        key_doc = jnp.take(doc_ids, key_pos)
        return (key_blk, value_blk, key_pos, key_doc)

    def stat_step(index, carry):
        running, total = carry
        key_blk, value_blk, key_pos, key_doc = key_slices(index * block, block)
        scores, allowed = score_block(queries, own_pos, own_doc, key_blk, key_pos, key_doc, scaling)
        newmax = jnp.maximum(running, jnp.max(jnp.where(allowed, scores, -1e30), axis=-1))
        total = total * jnp.exp(running - newmax) + jnp.sum(
            jnp.where(allowed, jnp.exp(scores - newmax[:, :, None]), 0.0), axis=-1
        )
        return (newmax, total)

    start_max = jnp.full((head_count, shard_rows), -1e30, jnp.float32)
    start_sum = jnp.zeros((head_count, shard_rows), jnp.float32)
    running, total = lax.fori_loop(0, block_count, stat_step, (start_max, start_sum))
    lse = running + jnp.log(total)

    def out_step(index, accum):
        key_blk, value_blk, key_pos, key_doc = key_slices(index * block, block)
        scores, allowed = score_block(queries, own_pos, own_doc, key_blk, key_pos, key_doc, scaling)
        probs = probs_of(scores, allowed, lse)
        return accum + jnp.einsum(
            "hqk,khd->qhd", probs, value_blk, preferred_element_type=jnp.float32
        )

    zero_rows = jnp.zeros((shard_rows, head_count, head_size), jnp.float32)
    attn_out = lax.fori_loop(0, block_count, out_step, zero_rows).astype(jnp.bfloat16)
    delta_rows = jnp.sum(out_grad.astype(jnp.float32) * attn_out.astype(jnp.float32), axis=-1)
    delta = delta_rows.T

    def query_step(index, accum):
        key_blk, value_blk, key_pos, key_doc = key_slices(index * block, block)
        scores, allowed = score_block(queries, own_pos, own_doc, key_blk, key_pos, key_doc, scaling)
        probs = probs_of(scores, allowed, lse)
        dscores = dscores_of(probs, out_grad, value_blk, delta)
        return accum + jnp.einsum(
            "hqk,khd->qhd", dscores, key_blk, preferred_element_type=jnp.float32
        )

    query_grad = (scaling * lax.fori_loop(0, block_count, query_step, zero_rows)).astype(
        jnp.bfloat16
    )
    lse_all, delta_all = (
        lax.all_gather(lse.T, "ctx", axis=0, tiled=True),
        lax.all_gather(delta_rows, "ctx", axis=0, tiled=True),
    )
    query_blk = lax.all_gather(queries, "ctx", axis=0, tiled=True)
    grad_blk = lax.all_gather(out_grad, "ctx", axis=0, tiled=True)
    length = query_blk.shape[0]
    query_pos = positions(jnp.int32(0), length)
    query_doc = jnp.take(doc_ids, query_pos)
    lse_blk = lse_all.T
    delta_blk = delta_all.T
    scores, allowed = score_block(
        query_blk, query_pos, query_doc, key_vecs, own_pos, own_doc, scaling
    )
    probs = probs_of(scores, allowed, lse_blk)
    dscores = dscores_of(probs, grad_blk, value_vecs, delta_blk)
    key_accum = scaling * jnp.einsum(
        "hqk,qhd->khd", dscores, query_blk, preferred_element_type=jnp.float32
    )
    value_accum = jnp.einsum("hqk,qhd->khd", probs, grad_blk, preferred_element_type=jnp.float32)
    key_grad = key_accum.astype(jnp.bfloat16)
    value_grad = value_accum.astype(jnp.bfloat16)
    return (attn_out, query_grad, key_grad, value_grad)


def solution(mesh):
    return jax.shard_map(
        on_device,
        mesh=mesh,
        in_specs=(
            P(("grp", "ctx"), "head", None),
            P(("grp", "ctx"), "head", None),
            P(("grp", "ctx"), "head", None),
            P(("grp", "ctx"), "head", None),
            P("grp"),
        ),
        out_specs=(
            P(("grp", "ctx"), "head", None),
            P(("grp", "ctx"), "head", None),
            P(("grp", "ctx"), "head", None),
            P(("grp", "ctx"), "head", None),
        ),
        check_vma=False,
    )
```

profile of v0, /device:TPU:0, one launch (start us, length us, event | category | flops | bytes accessed | tf_op | source)
XLA Modules:
  0.0 294.1 jit_solution(10098897156930762609)
XLA Ops:
  16.3 8.4 %gather_fusion.4 = s32[1536]{0:T(1024)S(1)} fusion(s32[1536]{0:T(1024)S(1)} %copy-done, s32[2048]{0:T(1024)S(1)} %pad_clamp_fusion.3), kind=kCustom, calls=%fused_computation.4 | custom fusion | bytes 18432 | tf_op jit(solution)/shard_map/jit(_take)/gather | solution.py:118
  26.4 47.6 %all-gather.9.cloned.1.call-done = bf16[1536,8,128]{2,0,1:T(8,128)(2,1)} async-done(((bf16[192,8,128]{2,0,1:T(8,128)(2,1)}), bf16[1536,8,128]{2,0,1:T(8,128)(2,1)}) %all-gather.9.cloned.1.call-update) | async-done | bytes 3145744 | tf_op jit(solution)/shard_map/all_gather | solution.py:57
  74.0 38.8 %while.50 = (s32[]{:T(128)}, f32[8,192]{1,0:T(8,128)S(1)}, f32[8,192]{1,0:T(8,128)}, s32[1536]{0:T(1024)S(1)}, s32[192]{0:T(256)}, /*index=5*/bf16[1536,8,128]{2...) while((s32[]{:T(128)}, f32[8,192]{1,0:T(8,128)S(1)}, ...), condition=%wide.region_3.5_spmd.clone, body=%wide.region_0.4_spmd.clone.sunk | while | flops 310742464 | bytes 24594968 | solution.py:82
  75.3 6.3 %gather_fusion = s32[768]{0:T(1024)} fusion(s32[1536]{0:T(1024)S(1)} %get-tuple-element.1162, s32[1024]{0:T(1024)} %pad_clamp_fusion.8), kind=kCustom, calls=%fused_computation.clone.clone.1 | custom fusion | bytes 9216 | tf_op jit(solution)/shard_map/while/body/eval_jaxpr/jit(_take)/gather | solution.py:67
  83.8 4.6 %fusion.142 = (f32[8,192]{1,0:T(8,128)}, f32[8,768,192]{1,2,0:T(8,128)}) fusion(pred[192,768]{1,0:T(8,128)(4,1)} %compare_and_fusion.7, bf16[192,8,128]{2,0,1:T(8,128)(2,1)S(1)} %get-tuple-element.1165, bf16[1536,8,128]{2,0,1:T(8,128)(2,1)S(1)} %copy-done.1, s32[]{:T(128)S(6)} %select_n.841), kind=kOutput, calls=%fused_computation.10.clone.1 | convolution fusion | flops 305527296 | bytes 6838276 | tf_op jit(solution)/shard_map/while/body/eval_jaxpr/qhd,khd->hqk/dot_general | solution.py:27
  94.7 6.3 %gather_fusion = s32[768]{0:T(1024)} fusion(s32[1536]{0:T(1024)S(1)} %get-tuple-element.1162, s32[1024]{0:T(1024)} %pad_clamp_fusion.8), kind=kCustom, calls=%fused_computation.clone.clone.1 | custom fusion | bytes 9216 | tf_op jit(solution)/shard_map/while/body/eval_jaxpr/jit(_take)/gather | solution.py:67
  103.2 4.6 %fusion.142 = (f32[8,192]{1,0:T(8,128)}, f32[8,768,192]{1,2,0:T(8,128)}) fusion(pred[192,768]{1,0:T(8,128)(4,1)} %compare_and_fusion.7, bf16[192,8,128]{2,0,1:T(8,128)(2,1)S(1)} %get-tuple-element.1165, bf16[1536,8,128]{2,0,1:T(8,128)(2,1)S(1)} %copy-done.1, s32[]{:T(128)S(6)} %select_n.841), kind=kOutput, calls=%fused_computation.10.clone.1 | convolution fusion | flops 305527296 | bytes 6838276 | tf_op jit(solution)/shard_map/while/body/eval_jaxpr/qhd,khd->hqk/dot_general | solution.py:27
  114.3 21.0 %all-gather.7.cloned.1.call-done = bf16[1536,8,128]{2,1,0:T(8,128)(2,1)} async-done(((bf16[192,8,128]{2,1,0:T(8,128)(2,1)}), bf16[1536,8,128]{2,1,0:T(8,128)(2,1)}) %all-gather.7.cloned.1.call-update) | async-done | bytes 3145744 | tf_op jit(solution)/shard_map/all_gather | solution.py:58
  135.3 4.0 %copy.35 = bf16[1536,8,128]{2,0,1:T(8,128)(2,1)} copy(bf16[1536,8,128]{2,1,0:T(8,128)(2,1)} %all-gather.7.cloned.1.call-done) | data formatting | bytes 6291456
  139.4 21.8 %while.51 = (s32[]{:T(128)}, f32[192,8,128]{2,0,1:T(8,128)}, bf16[1536,8,128]{2,0,1:T(8,128)(2,1)}, s32[1536]{0:T(1024)S(1)}, s32[192]{0:T(256)}, /*index=5*/bf1...) while((s32[]{:T(128)}, f32[192,8,128]{2,0,1:T(8,128)}, ...), condition=%wide.region_5.7_spmd.clone, body=%wide.region_4.6_spmd.clone.sunk | while | flops 609578944 | bytes 5453768 | solution.py:94
  140.0 4.6 %gather_fusion.1 = s32[768]{0:T(1024)S(1)} fusion(s32[1536]{0:T(1024)S(1)} %get-tuple-element.1200, s32[1024]{0:T(1024)} %pad_clamp_fusion.9), kind=kCustom, calls=%fused_computation.1.clone.clone.1 | custom fusion | bytes 9216 | tf_op jit(solution)/shard_map/while/body/eval_jaxpr/jit(_take)/gather | solution.py:67
  146.1 4.1 %fusion.149 = f32[192,8,128]{2,0,1:T(8,128)} fusion(bf16[1536,8,128]{2,0,1:T(8,128)(2,1)} %get-tuple-element.1199, s32[]{:T(128)S(6)} %select_n.855, bf16[192,8,128]{2,0,1:T(8,128)(2,1)S(1)} %get-tuple-element.1203, f32[8,192]{1,0:T(8,128)} %get-tuple-element.1204, pred[192,768]{1,0:T(8,128)(4,1)} %compare_and_fusion.8, ...), kind=kOutput, calls=%fused_computation.49.clone.1 | convolution fusion | flops 609091584 | bytes 5268992 | tf_op jit(solution)/shard_map/while/body/eval_jaxpr/hqk,khd->qhd/dot_general | solution.py:89
  150.8 4.6 %gather_fusion.1 = s32[768]{0:T(1024)S(1)} fusion(s32[1536]{0:T(1024)S(1)} %get-tuple-element.1200, s32[1024]{0:T(1024)} %pad_clamp_fusion.9), kind=kCustom, calls=%fused_computation.1.clone.clone.1 | custom fusion | bytes 9216 | tf_op jit(solution)/shard_map/while/body/eval_jaxpr/jit(_take)/gather | solution.py:67
  156.9 4.3 %fusion.149 = f32[192,8,128]{2,0,1:T(8,128)} fusion(bf16[1536,8,128]{2,0,1:T(8,128)(2,1)} %get-tuple-element.1199, s32[]{:T(128)S(6)} %select_n.855, bf16[192,8,128]{2,0,1:T(8,128)(2,1)S(1)} %get-tuple-element.1203, f32[8,192]{1,0:T(8,128)} %get-tuple-element.1204, pred[192,768]{1,0:T(8,128)(4,1)} %compare_and_fusion.8, ...), kind=kOutput, calls=%fused_computation.49.clone.1 | convolution fusion | flops 609091584 | bytes 5268992 | tf_op jit(solution)/shard_map/while/body/eval_jaxpr/hqk,khd->qhd/dot_general | solution.py:89
  165.9 31.1 %all-gather = f32[8,192,8]{1,2,0:T(8,128)S(1)} all-gather(f32[1,192,8]{1,2,0:T(8,128)} %bitcast.99), channel_id=1, replica_groups=mesh['grp'=2,'ctx'=8,'head'=2] {'ctx'}, dimensions={0}, use_global_device_ids=true | all-gather | bytes 55296 | tf_op jit(solution)/shard_map/all_gather | solution.py:111
  200.1 30.8 %all-gather.1 = f32[8,192,8]{1,2,0:T(8,128)S(1)} all-gather(f32[1,192,8]{1,2,0:T(8,128)S(1)} %copy.48), channel_id=1, replica_groups=mesh['grp'=2,'ctx'=8,'head'=2] {'ctx'}, dimensions={0}, use_global_device_ids=true | all-gather | bytes 55296 | tf_op jit(solution)/shard_map/all_gather | solution.py:112
  233.1 31.8 %while.52 = (s32[]{:T(128)}, f32[192,8,128]{2,0,1:T(8,128)}, bf16[1536,8,128]{2,0,1:T(8,128)(2,1)S(1)}, s32[1536]{0:T(1024)S(1)}, s32[192]{0:T(256)}, /*index=5*...) while((s32[]{:T(128)}, f32[192,8,128]{2,0,1:T(8,128)}, ...), condition=%wide.region_8.10_spmd.clone, body=%wide.region_7.9_spmd.clone.sunk | while | flops 916287424 | bytes 16865244 | solution.py:107
  236.6 4.6 %gather_fusion.2 = s32[768]{0:T(1024)S(1)} fusion(s32[1536]{0:T(1024)S(1)} %get-tuple-element.1243, s32[1024]{0:T(1024)} %pad_clamp_fusion.10), kind=kCustom, calls=%fused_computation.2.clone.clone.1 | custom fusion | bytes 9216 | tf_op jit(solution)/shard_map/while/body/eval_jaxpr/jit(_take)/gather | solution.py:67
  242.7 6.2 %fusion.157 = f32[192,8,128]{2,0,1:T(8,128)} fusion(bf16[1536,8,128]{2,0,1:T(8,128)(2,1)S(1)} %get-tuple-element.1242, s32[]{:T(128)S(6)} %select_n.869, f32[8,768,192]{1,2,0:T(8,128)} %fusion.156, f32[8,192]{1,0:T(8,128)} %get-tuple-element.1249, f32[8,192]{1,0:T(8,128)} %get-tuple-element.1246, pred[192,768]{1,0:T(8,128)(4,1)} %compare_and_fusion.9, ...), kind=kOutput, calls=%fused_computation.83.clone.1 | convolution fusion | flops 613810176 | bytes 9995776 | tf_op jit(solution)/shard_map/while/body/eval_jaxpr/hqk,khd->qhd/dot_general | solution.py:103
  252.4 4.6 %gather_fusion.2 = s32[768]{0:T(1024)S(1)} fusion(s32[1536]{0:T(1024)S(1)} %get-tuple-element.1243, s32[1024]{0:T(1024)} %pad_clamp_fusion.10), kind=kCustom, calls=%fused_computation.2.clone.clone.1 | custom fusion | bytes 9216 | tf_op jit(solution)/shard_map/while/body/eval_jaxpr/jit(_take)/gather | solution.py:67
  258.6 6.3 %fusion.157 = f32[192,8,128]{2,0,1:T(8,128)} fusion(bf16[1536,8,128]{2,0,1:T(8,128)(2,1)S(1)} %get-tuple-element.1242, s32[]{:T(128)S(6)} %select_n.869, f32[8,768,192]{1,2,0:T(8,128)} %fusion.156, f32[8,192]{1,0:T(8,128)} %get-tuple-element.1249, f32[8,192]{1,0:T(8,128)} %get-tuple-element.1246, pred[192,768]{1,0:T(8,128)(4,1)} %compare_and_fusion.9, ...), kind=kOutput, calls=%fused_computation.83.clone.1 | convolution fusion | flops 613810176 | bytes 9995776 | tf_op jit(solution)/shard_map/while/body/eval_jaxpr/hqk,khd->qhd/dot_general | solution.py:103
  267.3 6.7 %select_convert_fusion = bf16[8,1536,192]{1,2,0:T(8,128)(2,1)} fusion(bf16[1536,8,128]{2,0,1:T(8,128)(2,1)} %all-gather.11.cloned.1.call-done, f32[8,1536]{1,0:T(8,128)} %bitcast.97, pred[1536,192]{0,1:T(8,128)(4,1)} %compare_and_fusion.3, bf16[192,8,128]{2,1,0:T(8,128)(2,1)} %param.14), kind=kOutput, calls=%fused_computation.107 | convolution fusion | flops 613416960 | bytes 8601600 | tf_op jit(solution)/shard_map/qhd,khd->hqk/dot_general | solution.py:27
  274.0 6.9 %fusion.97 = bf16[192,8,128]{2,0,1:T(8,128)(2,1)S(1)} fusion(bf16[1536,8,128]{2,0,1:T(8,128)(2,1)} %all-gather.11.cloned.1.call-done, bf16[8,1536,192]{1,2,0:T(8,128)(2,1)} %select_convert_fusion, bf16[1536,8,128]{2,0,1:T(8,128)(2,1)} %all-gather.13.cloned.1.call-done, f32[8,1536]{1,0:T(8,128)S(1)} %bitcast.98, bf16[192,8,128]{2,1,0:T(8,128)(2,1)S(1)} %copy-done.4), kind=kOutput, calls=%fused_computation.113 | convolution fusion | flops 1217789952 | bytes 11845632 | tf_op jit(solution)/shard_map/hqk,qhd->khd/dot_general | solution.py:126
  281.9 4.7 %fusion.96 = bf16[192,8,128]{2,0,1:T(8,128)(2,1)S(1)} fusion(bf16[8,1536,192]{1,2,0:T(8,128)(2,1)} %select_convert_fusion, bf16[1536,8,128]{2,0,1:T(8,128)(2,1)} %all-gather.13.cloned.1.call-done), kind=kOutput, calls=%fused_computation.112 | convolution fusion | flops 604176384 | bytes 8257536 | tf_op jit(solution)/shard_map/hqk,qhd->khd/dot_general | solution.py:129
  (99 shorter events, 57.9 us)
Async XLA Ops:
  7.2 9.2 %copy-start = (s32[1536]{0:T(1024)S(1)}, s32[1536]{0:T(1024)}, u32[]{:S(2)}) copy-start(s32[1536]{0:T(1024)} %param.17) | copy-start | bytes 18436
  7.2 66.9 %all-gather.9.cloned.1.call-start = ((), (), s32[]{:S(2)}) async-start(), calls=%async_computation.1 | async-start | bytes 3538944 | tf_op jit(solution)/shard_map/all_gather | solution.py:57
  9.0 126.3 %all-gather.7.cloned.1.call-start = ((), (), s32[]{:S(2)}) async-start(), calls=%async_computation | async-start | bytes 3538944 | tf_op jit(solution)/shard_map/all_gather | solution.py:58
  9.8 257.5 %all-gather.11.cloned.1.call-start = ((), (), s32[]{:S(2)}) async-start(), calls=%async_computation.2 | async-start | bytes 3538944 | tf_op jit(solution)/shard_map/all_gather | solution.py:114
  11.7 262.3 %all-gather.13.cloned.1.call-start = ((), (), s32[]{:S(2)}) async-start(), calls=%async_computation.3 | async-start | bytes 3538944 | tf_op jit(solution)/shard_map/all_gather | solution.py:115
  13.8 60.3 %copy-start.3 = (bf16[192,8,128]{2,0,1:T(8,128)(2,1)S(1)}, bf16[192,8,128]{2,0,1:T(8,128)(2,1)}, u32[]{:S(2)}) copy-start(bf16[192,8,128]{2,0,1:T(8,128)(2,1)} %copy.36) | copy-start | bytes 1179652
  74.0 9.8 %copy-start.1 = (bf16[1536,8,128]{2,0,1:T(8,128)(2,1)S(1)}, bf16[1536,8,128]{2,0,1:T(8,128)(2,1)}, u32[]{:S(2)}) copy-start(bf16[1536,8,128]{2,0,1:T(8,128)(2,1)} %get-tuple-element.1164) | copy-start | bytes 9437188 | tf_op jit(solution)/shard_map/while
  88.4 4.4 %copy-start.5 = (f32[8,192]{1,0:T(8,128)S(1)}, f32[8,192]{1,0:T(8,128)}, u32[]{:S(2)}) copy-start(f32[8,192]{1,0:T(8,128)} %get-tuple-element.1149) | copy-start | bytes 18436 | tf_op jit(solution)/shard_map/while
  92.9 0.6 copy-start.6
  93.5 9.8 %copy-start.1 = (bf16[1536,8,128]{2,0,1:T(8,128)(2,1)S(1)}, bf16[1536,8,128]{2,0,1:T(8,128)(2,1)}, u32[]{:S(2)}) copy-start(bf16[1536,8,128]{2,0,1:T(8,128)(2,1)} %get-tuple-element.1164) | copy-start | bytes 9437188 | tf_op jit(solution)/shard_map/while
  107.8 4.4 %copy-start.5 = (f32[8,192]{1,0:T(8,128)S(1)}, f32[8,192]{1,0:T(8,128)}, u32[]{:S(2)}) copy-start(f32[8,192]{1,0:T(8,128)} %get-tuple-element.1149) | copy-start | bytes 18436 | tf_op jit(solution)/shard_map/while
  112.3 0.6 copy-start.6
  112.9 26.5 %copy-start.2 = (bf16[1536,8,128]{2,0,1:T(8,128)(2,1)S(1)}, bf16[1536,8,128]{2,0,1:T(8,128)(2,1)}, u32[]{:S(2)}) copy-start(bf16[1536,8,128]{2,0,1:T(8,128)(2,1)} %get-tuple-element.1262) | copy-start | bytes 9437188
  267.2 6.7 %copy-start.4 = (bf16[192,8,128]{2,1,0:T(8,128)(2,1)S(1)}, bf16[192,8,128]{2,1,0:T(8,128)(2,1)}, u32[]{:S(2)}) copy-start(bf16[192,8,128]{2,1,0:T(8,128)(2,1)} %param.15) | copy-start | bytes 1179652
  267.3 6.7 %copy-start.7 = (f32[1536,8]{0,1:T(8,128)S(1)}, f32[1536,8]{0,1:T(8,128)}, u32[]{:S(2)}) copy-start(f32[1536,8]{0,1:T(8,128)} %reshape.579) | copy-start | bytes 147460
Sparse Core Ops, SparseCore 0:
  10.8 63.2 all-gather.8
  76.2 59.0 all-gather.6
  138.1 60.3 all-gather.10
  200.5 59.2 all-gather.12
where the time goes:
time: 295 us; the launch traced here: 294 us
  waiting for transfers between devices  69.4 us (24%)
  blocking collectives  61.9 us (21%)
  local copies, waits for them, and re-layouts  60.9 us (21%)
  matrix products  54.1 us (18%)
  other arithmetic  33.7 us (11%)
  between operations  13.9 us (5%)
    all_gather x1, waiting for transfers between devices, on_device(): lax.all_gather(key_vecs, 'ctx', axis=0, tiled=True)  47.6 us
    all_gather x1, blocking collectives, on_device(): lax.all_gather(lse.T, 'ctx', axis=0, tiled=True)  31.1 us
    gather x6, local copies, waits for them, and re-layouts, key_slices(): key_doc = jnp.take(doc_ids, key_pos)  30.9 us
    all_gather x1, blocking collectives, on_device(): lax.all_gather(delta_rows, 'ctx', axis=0, tiled=True)  30.8 us
    dot_general x5, matrix products, score_block(): jnp.einsum('qhd,khd->hqk', query_blk, key_blk, preferred_element_type=jnp...  21.7 us
    all_gather x1, waiting for transfers between devices, on_device(): lax.all_gather(value_vecs, 'ctx', axis=0, tiled=True)  21 us
    unnamed x20, local copies, waits for them, and re-layouts  17.1 us
    dot_general x2, matrix products, query_step(): jnp.einsum('hqk,khd->qhd', dscores, key_blk, preferred_element_type=jnp.f...  12.5 us
  transfers between devices with their start and end apart: 4, of which 2 were waited for; matrix products, arithmetic and copies ran while one was open for 45% of the time, Pallas kernels for 0%

commit v1 on v0

--- a/solution.py
+++ b/solution.py
@@ -1,6 +1,10 @@
+import functools
+
 import jax
 import jax.numpy as jnp
 from jax import lax
+from jax.experimental import pallas as pl
+from jax.experimental.pallas import tpu as pltpu
 from jax.sharding import PartitionSpec as P
 
 
@@ -39,7 +43,7 @@
     return (probs.astype(jnp.float32) * (dprobs - delta[:, :, None])).astype(jnp.bfloat16)
 
 
-def on_device(queries, key_vecs, value_vecs, out_grad, doc_ids):
+def gathered(queries, key_vecs, value_vecs, out_grad, doc_ids):
     shard_rows = queries.shape[0]
     head_count = queries.shape[1]
     head_size = queries.shape[2]
@@ -132,6 +136,302 @@
     return (attn_out, query_grad, key_grad, value_grad)
 
 
+KEY, QUERY, VALUE, GRAD = 0, 1, 2, 3
+OUT, DQ, DK, DV = 0, 1, 2, 3
+LOG2E = 1.4426950408889634
+
+
+def nt_dot(a, b):
+    return lax.dot_general(a, b, (((1,), (1,)), ((), ())), preferred_element_type=jnp.float32)
+
+
+def head_kernel(
+    shards,
+    half,
+    group,
+    key_ref,
+    query_ref,
+    value_ref,
+    grad_ref,
+    doc_ref,
+    out_ref,
+    staged,
+    wide,
+    full,
+    ready,
+    doc_col,
+    key_t,
+    value_t,
+    out_t,
+    score_buf,
+    prob_buf,
+    key_acc,
+    value_acc,
+    in_send,
+    in_recv,
+    out_send,
+    out_recv,
+):
+    me = lax.axis_index("ctx")
+    size = half * group
+    blocks = 2 * shards // group
+    head_size = full.shape[-1]
+    scaling = head_size ** (-0.5)
+
+    barrier = pltpu.get_barrier_semaphore()
+
+    def greet(step, carry):
+        pl.semaphore_signal(
+            barrier,
+            inc=1,
+            device_id={"ctx": lax.rem(me + step, shards)},
+            device_id_type=pl.DeviceIdType.MESH,
+        )
+        return carry
+
+    lax.fori_loop(1, shards, greet, 0)
+
+    def stage(kind, ref):
+        rows = ref.shape[0]
+        wide[...] = ref[...].astype(jnp.float32).reshape(rows * shards, head_size)
+        for head in range(shards):
+            staged[kind, head] = wide[pl.ds(head, rows, stride=shards), :].astype(jnp.bfloat16)
+
+    def part_rows(part):
+        return pl.ds(part * half, half)
+
+    def block_rows(index):
+        return pl.ds(pl.multiple_of(index * half, half), half)
+
+    def position(part):
+        return me if part == 0 else 2 * shards - 1 - me
+
+    def send_in(kind, part):
+        where = position(part)
+        pltpu.make_async_copy(
+            staged.at[kind, me, part_rows(part)],
+            full.at[kind, block_rows(where)],
+            in_recv.at[kind, where],
+        ).start()
+
+        def one(step, carry):
+            target = lax.rem(me + step, shards)
+            pltpu.make_async_remote_copy(
+                src_ref=staged.at[kind, target, part_rows(part)],
+                dst_ref=full.at[kind, block_rows(where)],
+                send_sem=in_send.at[kind, part, step],
+                recv_sem=in_recv.at[kind, where],
+                device_id={"ctx": target},
+                device_id_type=pl.DeviceIdType.MESH,
+            ).start()
+            return carry
+
+        lax.fori_loop(1, shards, one, 0)
+
+    def wait_in(kind, block):
+        def one(index, carry):
+            held = full.at[kind, block_rows(index)]
+            pltpu.make_async_copy(held, held, in_recv.at[kind, index]).wait()
+            return carry
+
+        lax.fori_loop(block * group, (block + 1) * group, one, 0)
+
+    def send_out(kind, block):
+        for index in range(block * group, (block + 1) * group):
+            part = 0 if index < shards else 1
+            owner = index if part == 0 else 2 * shards - 1 - index
+            held = ready.at[kind, pl.ds(index * half, half)]
+            place = out_ref.at[kind, me, part_rows(part)]
+
+            @pl.when(owner == me)
+            def _():
+                pltpu.make_async_copy(held, place, out_recv.at[kind, part, me]).start()
+
+            @pl.when(owner != me)
+            def _():
+                pltpu.make_async_remote_copy(
+                    src_ref=held,
+                    dst_ref=place,
+                    send_sem=out_send.at[kind, index],
+                    recv_sem=out_recv.at[kind, part, me],
+                    device_id={"ctx": owner},
+                    device_id_type=pl.DeviceIdType.MESH,
+                ).start()
+
+    stage(KEY, key_ref)
+    stage(QUERY, query_ref)
+    pl.semaphore_wait(barrier, shards - 1)
+    send_in(KEY, 0)
+    send_in(QUERY, 0)
+    stage(VALUE, value_ref)
+    send_in(VALUE, 0)
+    send_in(KEY, 1)
+    send_in(QUERY, 1)
+    send_in(VALUE, 1)
+    stage(GRAD, grad_ref)
+    send_in(GRAD, 1)
+    send_in(GRAD, 0)
+
+    docs = doc_ref[...].astype(jnp.float32)
+    for block in range(blocks):
+        piece = docs[:, block * size : (block + 1) * size]
+        doc_col[block] = jnp.broadcast_to(piece, (128, size)).T
+
+    def rows_of(block):
+        return pl.ds(block * size, size)
+
+    for block in range(blocks):
+        wait_in(KEY, block)
+        wait_in(QUERY, block)
+        queries = full[QUERY, rows_of(block)]
+        query_doc = docs[:, block * size : (block + 1) * size]
+        largest = None
+        for other in range(block + 1):
+            scores = nt_dot(full[KEY, rows_of(other)], queries)
+            key_doc = jnp.concatenate([doc_col[other]] * (size // 128), axis=1)
+            seen = key_doc == query_doc
+            if other == block:
+                key_at = lax.broadcasted_iota(jnp.int32, (size, size), 0)
+                query_at = lax.broadcasted_iota(jnp.int32, (size, size), 1)
+                seen = seen & (key_at <= query_at)
+            scores = jnp.where(seen, scores, -1e30)
+            score_buf[other] = scores
+            top = jnp.max(scores, axis=0, keepdims=True)
+            largest = top if largest is None else jnp.maximum(largest, top)
+        total = jnp.zeros((1, size), jnp.float32)
+        for other in range(block + 1):
+            weights = jnp.exp2((score_buf[other] - largest) * (scaling * LOG2E))
+            score_buf[other] = weights
+            total = total + jnp.sum(weights, axis=0, keepdims=True)
+        inverse = 1.0 / total
+        wait_in(VALUE, block)
+        value_t[block] = full[VALUE, rows_of(block)].astype(jnp.float32).T.astype(jnp.bfloat16)
+        key_t[block] = full[KEY, rows_of(block)].astype(jnp.float32).T.astype(jnp.bfloat16)
+        accum = jnp.zeros((head_size, size), jnp.float32)
+        for other in range(block + 1):
+            probs = (score_buf[other] * inverse).astype(jnp.bfloat16)
+            prob_buf[block, other] = probs
+            accum = accum + jnp.dot(value_t[other], probs, preferred_element_type=jnp.float32)
+        rounded = accum.astype(jnp.bfloat16).astype(jnp.float32)
+        out_t[block] = rounded
+        ready[OUT, rows_of(block)] = rounded.T.astype(jnp.bfloat16)
+        send_out(OUT, block)
+
+    for block in reversed(range(blocks)):
+        wait_in(GRAD, block)
+        queries = full[QUERY, rows_of(block)]
+        grads = full[GRAD, rows_of(block)]
+        delta = jnp.sum(grads.astype(jnp.float32).T * out_t[block], axis=0, keepdims=True)
+        accum = jnp.zeros((head_size, size), jnp.float32)
+        for other in range(block + 1):
+            probs = prob_buf[block, other]
+            dprobs = nt_dot(full[VALUE, rows_of(other)], grads)
+            dscores = (probs.astype(jnp.float32) * (dprobs - delta)).astype(jnp.bfloat16)
+            value_part = jnp.dot(probs, grads, preferred_element_type=jnp.float32)
+            key_part = jnp.dot(dscores, queries, preferred_element_type=jnp.float32)
+            if block < blocks - 1:
+                value_part = value_part + value_acc[other]
+                key_part = key_part + key_acc[other]
+            if other < block:
+                value_acc[other] = value_part
+                key_acc[other] = key_part
+            else:
+                ready[DV, rows_of(block)] = value_part.astype(jnp.bfloat16)
+                ready[DK, rows_of(block)] = (scaling * key_part).astype(jnp.bfloat16)
+            accum = accum + jnp.dot(key_t[other], dscores, preferred_element_type=jnp.float32)
+        ready[DQ, rows_of(block)] = (scaling * accum).T.astype(jnp.bfloat16)
+        for kind in (DV, DK, DQ):
+            send_out(kind, block)
+
+    def drain(step, carry):
+        target = lax.rem(me + step, shards)
+        for kind in range(4):
+            for part in range(2):
+                left = staged.at[kind, target, part_rows(part)]
+                pltpu.make_async_copy(left, left, in_send.at[kind, part, step]).wait()
+        return carry
+
+    lax.fori_loop(1, shards, drain, 0)
+
+    def drain_out(index, carry):
+        owner = jnp.where(index < shards, index, 2 * shards - 1 - index)
+
+        @pl.when(owner != me)
+        def _():
+            for kind in range(4):
+                left = ready.at[kind, block_rows(index)]
+                pltpu.make_async_copy(left, left, out_send.at[kind, index]).wait()
+
+        return carry
+
+    lax.fori_loop(0, 2 * shards, drain_out, 0)
+
+    def collect(source, carry):
+        for kind in range(4):
+            for part in range(2):
+                place = out_ref.at[kind, source, part_rows(part)]
+                pltpu.make_async_copy(place, place, out_recv.at[kind, part, source]).wait()
+        return carry
+
+    lax.fori_loop(0, shards, collect, 0)
+
+
+def by_heads(queries, key_vecs, value_vecs, out_grad, doc_ids):
+    shard_rows, head_count, head_size = queries.shape
+    shards = lax.axis_size("ctx")
+    half = shard_rows // 2
+    tokens = shard_rows * shards
+    group = 4
+    size = group * half
+    blocks = tokens // size
+    bf16, f32 = jnp.bfloat16, jnp.float32
+    vmem = pl.BlockSpec(memory_space=pltpu.VMEM)
+    flops = 7 * tokens * tokens * head_size
+    results = pl.pallas_call(
+        functools.partial(head_kernel, shards, half, group),
+        out_shape=jax.ShapeDtypeStruct((4, shards, shard_rows, head_size), bf16),
+        in_specs=[vmem] * 5,
+        out_specs=pl.BlockSpec(memory_space=pl.ANY),
+        scratch_shapes=[
+            pltpu.VMEM((4, shards, shard_rows, head_size), bf16),
+            pltpu.VMEM((tokens, head_size), f32),
+            pltpu.VMEM((4, tokens, head_size), bf16),
+            pltpu.VMEM((4, tokens, head_size), bf16),
+            pltpu.VMEM((blocks, size, 128), f32),
+            pltpu.VMEM((blocks, head_size, size), bf16),
+            pltpu.VMEM((blocks, head_size, size), bf16),
+            pltpu.VMEM((blocks, head_size, size), f32),
+            pltpu.VMEM((blocks, size, size), f32),
+            pltpu.VMEM((blocks, blocks, size, size), bf16),
+            pltpu.VMEM((blocks, size, head_size), f32),
+            pltpu.VMEM((blocks, size, head_size), f32),
+            pltpu.SemaphoreType.DMA((4, 2, shards)),
+            pltpu.SemaphoreType.DMA((4, 2 * shards)),
+            pltpu.SemaphoreType.DMA((4, 2 * shards)),
+            pltpu.SemaphoreType.DMA((4, 2, shards)),
+        ],
+        compiler_params=pltpu.CompilerParams(
+            collective_id=0, has_side_effects=True, vmem_limit_bytes=40 * 1024 * 1024
+        ),
+        cost_estimate=pl.CostEstimate(
+            flops=flops, bytes_accessed=8 * queries.size * 2, transcendentals=tokens * tokens // 2
+        ),
+    )(key_vecs, queries, value_vecs, out_grad, doc_ids.reshape(1, tokens))
+    return tuple(jnp.swapaxes(results[kind], 0, 1) for kind in range(4))
+
+
+def on_device(queries, key_vecs, value_vecs, out_grad, doc_ids):
+    shard_rows, head_count, head_size = queries.shape
+    fits = (
+        head_count == lax.axis_size("ctx")
+        and shard_rows % 32 == 0
+        and (2 * shard_rows) % 128 == 0
+        and head_size == 128
+    )
+    attend = by_heads if fits else gathered
+    return attend(queries, key_vecs, value_vecs, out_grad, doc_ids)
+
+
 def solution(mesh):
     return jax.shard_map(
         on_device,

time: 295 us -> 85.1 us (0.29)
  Pallas kernels: 0 us -> 75.3 us
  waiting for transfers between devices: 69.4 us -> 0 us
  blocking collectives: 61.9 us -> 0 us
  matrix products: 54.1 us -> 0 us
  local copies, waits for them, and re-layouts: 60.9 us -> 8.8 us
  other arithmetic: 33.7 us -> 0 us
  between operations: 13.9 us -> 0.65 us
    pallas_call x0 -> x1, Pallas kernels: none -> 75.3 us  [by_heads(): pl.pallas_call(functools.partial(head_kernel, shards, half, group), out_s...]
    all_gather x4 -> x0, waiting for transfers between devices: 68.6 us -> none  [the longest x1 47.6 us: on_device(): lax.all_gather(key_vecs, 'ctx', axis=0, tiled=True)]
    all_gather x2 -> x0, blocking collectives: 61.9 us -> none  [the longest x1 31.1 us: on_device(): lax.all_gather(lse.T, 'ctx', axis=0, tiled=True)]
    dot_general x11 -> x0, matrix products: 54.1 us -> none  [the longest x5 21.7 us: score_block(): jnp.einsum('qhd,khd->hqk', query_blk, key_blk, preferred_element_type=jnp...]
    gather x8 -> x0, local copies, waits for them, and re-layouts: 41.3 us -> none  [the longest x6 30.9 us: key_slices(): key_doc = jnp.take(doc_ids, key_pos)]
    and x7 -> x0, other arithmetic: 10.7 us -> none  [score_block(): (key_doc[None, :] == query_doc[:, None]) & (key_pos[None, :] <= query_pos...]
    reduce_sum x3 -> x0, other arithmetic: 10.5 us -> none  [the longest x2 7.37 us: stat_step(): jnp.sum(jnp.where(allowed, jnp.exp(scores - newmax[:, :, None]), 0.0), ax...]
    unnamed x20 -> x12, local copies, waits for them, and re-layouts: 17.1 us -> 7.99 us
  transfers between devices with their start and end apart: 4 -> 0, of which waited for: 2 -> 0; matrix products, arithmetic and copies ran while one was open for 45% -> 0% of each run, Pallas kernels for 0% -> 0%
where the time goes in v1:
time: 85.1 us; the launch traced here: 84.8 us
  Pallas kernels  75.3 us (88%)
  local copies, waits for them, and re-layouts  8.8 us (10%)
    pallas_call x1, Pallas kernels, by_heads(): pl.pallas_call(functools.partial(head_kernel, shards, half, group), out_s...  75.3 us
    unnamed x12, local copies, waits for them, and re-layouts  7.99 us

profile of v1, /device:TPU:0, one launch (start us, length us, event | category | flops | bytes accessed | tf_op | source)
XLA Modules:
  0.0 84.8 jit_solution(13257280417359960093)
XLA Ops:
  0.6 0.7 reshape.11.doc_ref
  1.3 0.0 copy-start
  1.3 1.0 %copy-done = bf16[192,8,128]{2,1,0:T(8,128)(2,1)S(1)} copy-done((bf16[192,8,128]{2,1,0:T(8,128)(2,1)S(1)}, bf16[192,8,128]{2,1,0:T(8,128)(2,1)}, u32[]{:S(2)}) %copy-start) | copy-done | bytes 393240
  2.3 0.0 copy-start.1
  2.3 1.0 %copy-done.1 = bf16[192,8,128]{2,1,0:T(8,128)(2,1)S(1)} copy-done((bf16[192,8,128]{2,1,0:T(8,128)(2,1)S(1)}, bf16[192,8,128]{2,1,0:T(8,128)(2,1)}, u32[]{:S(2)}) %copy-start.1) | copy-done | bytes 393240
  3.3 0.0 copy-start.2
  3.3 1.0 %copy-done.2 = bf16[192,8,128]{2,1,0:T(8,128)(2,1)S(1)} copy-done((bf16[192,8,128]{2,1,0:T(8,128)(2,1)S(1)}, bf16[192,8,128]{2,1,0:T(8,128)(2,1)}, u32[]{:S(2)}) %copy-start.2) | copy-done | bytes 393240
  4.3 0.0 copy-start.3
  4.3 1.0 %copy-done.3 = bf16[192,8,128]{2,1,0:T(8,128)(2,1)S(1)} copy-done((bf16[192,8,128]{2,1,0:T(8,128)(2,1)S(1)}, bf16[192,8,128]{2,1,0:T(8,128)(2,1)}, u32[]{:S(2)}) %copy-start.3) | copy-done | bytes 393240
  5.3 75.3 %shard_map.84 = bf16[4,8,192,128]{3,2,1,0:T(8,128)(2,1)S(1)} custom-call(bf16[192,8,128]{2,1,0:T(8,128)(2,1)S(1)} %copy-done, bf16[192,8,128]{2,1,0:T(8,128)(2,1)S(1)} %copy-done.1, bf16[192,8,128]{2,1,0:T(8,128)(2,1)S(1)} %copy-done.2, bf16[192,8,128]{2,1,0:T(8,128)(2,1)S(1)} %copy-done.3, s32[1,1536]{1,0:T(1,128)S(1)} %reshape.11.doc_ref), custom_call_target="tpu_custom_call" | custom-call | flops 2113929216 | bytes 3145728 | tf_op jit(solution)/shard_map/pallas_call | solution.py:390
  80.6 0.1 slice_bitcast_fusion
  80.8 1.0 %copy.12 = bf16[192,8,128]{2,1,0:T(8,128)(2,1)} copy(bf16[192,8,128]{2,0,1:T(8,128)(2,1)S(1)} %get-tuple-element.8) | data formatting | bytes 786432
  81.8 1.0 %copy.11 = bf16[192,8,128]{2,1,0:T(8,128)(2,1)} copy(bf16[192,8,128]{2,0,1:T(8,128)(2,1)S(1)} %get-tuple-element.9) | data formatting | bytes 786432
  82.8 1.0 %copy.10 = bf16[192,8,128]{2,1,0:T(8,128)(2,1)} copy(bf16[192,8,128]{2,0,1:T(8,128)(2,1)S(1)} %get-tuple-element.10) | data formatting | bytes 786432
  83.8 1.0 %copy.9 = bf16[192,8,128]{2,1,0:T(8,128)(2,1)} copy(bf16[192,8,128]{2,0,1:T(8,128)(2,1)S(1)} %get-tuple-element.11) | data formatting | bytes 786432
Async XLA Ops:
  1.3 1.0 %copy-start = (bf16[192,8,128]{2,1,0:T(8,128)(2,1)S(1)}, bf16[192,8,128]{2,1,0:T(8,128)(2,1)}, u32[]{:S(2)}) copy-start(bf16[192,8,128]{2,1,0:T(8,128)(2,1)} %key_ref.1) | copy-start | bytes 1179652
  2.3 1.0 %copy-start.1 = (bf16[192,8,128]{2,1,0:T(8,128)(2,1)S(1)}, bf16[192,8,128]{2,1,0:T(8,128)(2,1)}, u32[]{:S(2)}) copy-start(bf16[192,8,128]{2,1,0:T(8,128)(2,1)} %query_ref.1) | copy-start | bytes 1179652
  3.3 1.0 %copy-start.2 = (bf16[192,8,128]{2,1,0:T(8,128)(2,1)S(1)}, bf16[192,8,128]{2,1,0:T(8,128)(2,1)}, u32[]{:S(2)}) copy-start(bf16[192,8,128]{2,1,0:T(8,128)(2,1)} %value_ref.1) | copy-start | bytes 1179652
  4.3 1.0 %copy-start.3 = (bf16[192,8,128]{2,1,0:T(8,128)(2,1)S(1)}, bf16[192,8,128]{2,1,0:T(8,128)(2,1)}, u32[]{:S(2)}) copy-start(bf16[192,8,128]{2,1,0:T(8,128)(2,1)} %grad_ref.1) | copy-start | bytes 1179652

commit v2 on v1

--- a/solution.py
+++ b/solution.py
@@ -155,6 +155,7 @@
     grad_ref,
     doc_ref,
     out_ref,
+    fetched,
     staged,
     wide,
     full,
@@ -171,12 +172,20 @@
     in_recv,
     out_send,
     out_recv,
+    fetch_sem,
 ):
     me = lax.axis_index("ctx")
     size = half * group
     blocks = 2 * shards // group
     head_size = full.shape[-1]
     scaling = head_size ** (-0.5)
+
+    fetches = [
+        pltpu.make_async_copy(ref, fetched.at[kind], fetch_sem.at[kind])
+        for kind, ref in ((KEY, key_ref), (QUERY, query_ref), (VALUE, value_ref), (GRAD, grad_ref))
+    ]
+    for fetch in fetches:
+        fetch.start()
 
     barrier = pltpu.get_barrier_semaphore()
 
@@ -191,9 +200,10 @@
 
     lax.fori_loop(1, shards, greet, 0)
 
-    def stage(kind, ref):
-        rows = ref.shape[0]
-        wide[...] = ref[...].astype(jnp.float32).reshape(rows * shards, head_size)
+    def stage(kind):
+        fetches[kind].wait()
+        rows = fetched.shape[1]
+        wide[...] = fetched[kind].astype(jnp.float32).reshape(rows * shards, head_size)
         for head in range(shards):
             staged[kind, head] = wide[pl.ds(head, rows, stride=shards), :].astype(jnp.bfloat16)
 
@@ -205,6 +215,17 @@
 
     def position(part):
         return me if part == 0 else 2 * shards - 1 - me
+
+    def far_first(step):
+        return lax.rem(step + shards // 2 - 2, shards - 1) + 1
+
+    def sent_in(kind, part):
+        def one(step, carry):
+            left = staged.at[kind, lax.rem(me + far_first(step), shards), part_rows(part)]
+            pltpu.make_async_copy(left, left, in_send.at[kind, part, step]).wait()
+            return carry
+
+        lax.fori_loop(1, shards, one, 0)
 
     def send_in(kind, part):
         where = position(part)
@@ -215,7 +236,7 @@
         ).start()
 
         def one(step, carry):
-            target = lax.rem(me + step, shards)
+            target = lax.rem(me + far_first(step), shards)
             pltpu.make_async_remote_copy(
                 src_ref=staged.at[kind, target, part_rows(part)],
                 dst_ref=full.at[kind, block_rows(where)],
@@ -258,29 +279,32 @@
                     device_id_type=pl.DeviceIdType.MESH,
                 ).start()
 
-    stage(KEY, key_ref)
-    stage(QUERY, query_ref)
+    stage(KEY)
     pl.semaphore_wait(barrier, shards - 1)
     send_in(KEY, 0)
+    stage(QUERY)
     send_in(QUERY, 0)
-    stage(VALUE, value_ref)
+    stage(VALUE)
     send_in(VALUE, 0)
-    send_in(KEY, 1)
-    send_in(QUERY, 1)
-    send_in(VALUE, 1)
-    stage(GRAD, grad_ref)
-    send_in(GRAD, 1)
-    send_in(GRAD, 0)
-
-    docs = doc_ref[...].astype(jnp.float32)
+    stage(GRAD)
+
+    docs = doc_ref[...].astype(jnp.float32).reshape(1, -1)
     for block in range(blocks):
         piece = docs[:, block * size : (block + 1) * size]
         doc_col[block] = jnp.broadcast_to(piece, (128, size)).T
 
+    for kind in (KEY, QUERY, VALUE):
+        sent_in(kind, 0)
+        send_in(kind, 1)
+
     def rows_of(block):
         return pl.ds(block * size, size)
 
     for block in range(blocks):
+        if block == blocks // 2:
+            for kind, part in ((KEY, 1), (QUERY, 0)):
+                sent_in(kind, 1)
+                send_in(GRAD, part)
         wait_in(KEY, block)
         wait_in(QUERY, block)
         queries = full[QUERY, rows_of(block)]
@@ -343,15 +367,8 @@
         for kind in (DV, DK, DQ):
             send_out(kind, block)
 
-    def drain(step, carry):
-        target = lax.rem(me + step, shards)
-        for kind in range(4):
-            for part in range(2):
-                left = staged.at[kind, target, part_rows(part)]
-                pltpu.make_async_copy(left, left, in_send.at[kind, part, step]).wait()
-        return carry
-
-    lax.fori_loop(1, shards, drain, 0)
+    for kind, part in ((VALUE, 1), (GRAD, 1), (GRAD, 0)):
+        sent_in(kind, part)
 
     def drain_out(index, carry):
         owner = jnp.where(index < shards, index, 2 * shards - 1 - index)
@@ -374,6 +391,28 @@
         return carry
 
     lax.fori_loop(0, shards, collect, 0)
+
+
+def rows_kernel(heads_ref, out_a, out_b, out_c, out_d, held, wide, turned, in_sem, out_sem):
+    heads, rows, head_size = held.shape[1:]
+    outs = (out_a, out_b, out_c, out_d)
+    reads = [
+        pltpu.make_async_copy(heads_ref.at[kind], held.at[kind], in_sem.at[kind])
+        for kind in range(4)
+    ]
+    writes = [
+        pltpu.make_async_copy(turned.at[kind], outs[kind], out_sem.at[kind]) for kind in range(4)
+    ]
+    for read in reads:
+        read.start()
+    for kind in range(4):
+        reads[kind].wait()
+        for head in range(heads):
+            wide[pl.ds(head, rows, stride=heads), :] = held[kind, head].astype(jnp.float32)
+        turned[kind] = wide[...].reshape(rows, heads, head_size).astype(jnp.bfloat16)
+        writes[kind].start()
+    for write in writes:
+        write.wait()
 
 
 def by_heads(queries, key_vecs, value_vecs, out_grad, doc_ids):
@@ -390,9 +429,10 @@
     results = pl.pallas_call(
         functools.partial(head_kernel, shards, half, group),
         out_shape=jax.ShapeDtypeStruct((4, shards, shard_rows, head_size), bf16),
-        in_specs=[vmem] * 5,
+        in_specs=[pl.BlockSpec(memory_space=pltpu.HBM)] * 4 + [vmem],
         out_specs=pl.BlockSpec(memory_space=pl.ANY),
         scratch_shapes=[
+            pltpu.VMEM((4, shard_rows, shards, head_size), bf16),
             pltpu.VMEM((4, shards, shard_rows, head_size), bf16),
             pltpu.VMEM((tokens, head_size), f32),
             pltpu.VMEM((4, tokens, head_size), bf16),
@@ -409,6 +449,7 @@
             pltpu.SemaphoreType.DMA((4, 2 * shards)),
             pltpu.SemaphoreType.DMA((4, 2 * shards)),
             pltpu.SemaphoreType.DMA((4, 2, shards)),
+            pltpu.SemaphoreType.DMA((4,)),
         ],
         compiler_params=pltpu.CompilerParams(
             collective_id=0, has_side_effects=True, vmem_limit_bytes=40 * 1024 * 1024
@@ -416,8 +457,25 @@
         cost_estimate=pl.CostEstimate(
             flops=flops, bytes_accessed=8 * queries.size * 2, transcendentals=tokens * tokens // 2
         ),
-    )(key_vecs, queries, value_vecs, out_grad, doc_ids.reshape(1, tokens))
-    return tuple(jnp.swapaxes(results[kind], 0, 1) for kind in range(4))
+    )(key_vecs, queries, value_vecs, out_grad, doc_ids)
+    rows_first = jax.ShapeDtypeStruct((shard_rows, shards, head_size), bf16)
+    return pl.pallas_call(
+        rows_kernel,
+        out_shape=[rows_first] * 4,
+        in_specs=[pl.BlockSpec(memory_space=pl.ANY)],
+        out_specs=[pl.BlockSpec(memory_space=pl.ANY)] * 4,
+        scratch_shapes=[
+            pltpu.VMEM((4, shards, shard_rows, head_size), bf16),
+            pltpu.VMEM((shard_rows * shards, head_size), f32),
+            pltpu.VMEM((4, shard_rows, shards, head_size), bf16),
+            pltpu.SemaphoreType.DMA((4,)),
+            pltpu.SemaphoreType.DMA((4,)),
+        ],
+        compiler_params=pltpu.CompilerParams(vmem_limit_bytes=16 * 1024 * 1024),
+        cost_estimate=pl.CostEstimate(
+            flops=0, bytes_accessed=16 * queries.size, transcendentals=0
+        ),
+    )(results)
 
 
 def on_device(queries, key_vecs, value_vecs, out_grad, doc_ids):

time: 85.1 us -> 84.8 us (level)
  local copies, waits for them, and re-layouts: 8.8 us -> 4.67 us
  Pallas kernels: 75.3 us -> 79.1 us
    unnamed x12 -> x10, local copies, waits for them, and re-layouts: 7.99 us -> 4.67 us
    pallas_call x0 -> x1, Pallas kernels: none -> 2.52 us  [by_heads(): pl.pallas_call(rows_kernel, out_shape=[rows_first] * 4, in_specs=[pl.Bloc...]
    pallas_call x1, Pallas kernels: 75.3 us -> 76.6 us  [by_heads(): pl.pallas_call(functools.partial(head_kernel, shards, half, group), out_s...]
where the time goes in v2:
time: 84.8 us; the launch traced here: 84.5 us
  Pallas kernels  79.1 us (93%)
  local copies, waits for them, and re-layouts  4.67 us (6%)
    pallas_call x1, Pallas kernels, by_heads(): pl.pallas_call(functools.partial(head_kernel, shards, half, group), out_s...  76.6 us
    unnamed x10, local copies, waits for them, and re-layouts  4.67 us
    pallas_call x1, Pallas kernels, by_heads(): pl.pallas_call(rows_kernel, out_shape=[rows_first] * 4, in_specs=[pl.Bloc...  2.52 us

profile of v2, /device:TPU:0, one launch (start us, length us, event | category | flops | bytes accessed | tf_op | source)
XLA Modules:
  0.0 84.5 jit_solution(3397400102941175126)
XLA Ops:
  0.6 0.0 copy-start
  0.6 1.0 %copy-done = bf16[192,8,128]{2,1,0:T(8,128)(2,1)S(1)} copy-done((bf16[192,8,128]{2,1,0:T(8,128)(2,1)S(1)}, bf16[192,8,128]{2,1,0:T(8,128)(2,1)}, u32[]{:S(2)}) %copy-start) | copy-done | bytes 393240
  1.6 0.0 copy-start.1
  1.6 1.0 %copy-done.1 = bf16[192,8,128]{2,1,0:T(8,128)(2,1)S(1)} copy-done((bf16[192,8,128]{2,1,0:T(8,128)(2,1)S(1)}, bf16[192,8,128]{2,1,0:T(8,128)(2,1)}, u32[]{:S(2)}) %copy-start.1) | copy-done | bytes 393240
  2.6 0.0 copy-start.2
  2.6 1.0 %copy-done.2 = bf16[192,8,128]{2,1,0:T(8,128)(2,1)S(1)} copy-done((bf16[192,8,128]{2,1,0:T(8,128)(2,1)S(1)}, bf16[192,8,128]{2,1,0:T(8,128)(2,1)}, u32[]{:S(2)}) %copy-start.2) | copy-done | bytes 393240
  3.6 0.0 copy-start.3
  3.6 1.0 %copy-done.3 = bf16[192,8,128]{2,1,0:T(8,128)(2,1)S(1)} copy-done((bf16[192,8,128]{2,1,0:T(8,128)(2,1)S(1)}, bf16[192,8,128]{2,1,0:T(8,128)(2,1)}, u32[]{:S(2)}) %copy-start.3) | copy-done | bytes 393240
  4.6 0.0 copy-start.4
  4.6 0.7 copy-done.4
  5.3 76.6 %shard_map.84.heads_ref = bf16[4,8,192,128]{3,2,1,0:T(8,128)(2,1)S(1)} custom-call(bf16[192,8,128]{2,1,0:T(8,128)(2,1)S(1)} %copy-done, bf16[192,8,128]{2,1,0:T(8,128)(2,1)S(1)} %copy-done.1, bf16[192,8,128]{2,1,0:T(8,128)(2,1)S(1)} %copy-done.2, bf16[192,8,128]{2,1,0:T(8,128)(2,1)S(1)} %copy-done.3, s32[1536]{0:T(1024)S(1)} %copy-done.4), custom_call_target="tpu_custom_call" | custom-call | flops 2113929216 | bytes 3145728 | tf_op jit(solution)/shard_map/pallas_call | solution.py:429
  81.9 2.5 %shard_map.85 = (bf16[192,8,128]{2,1,0:T(8,128)(2,1)}, bf16[192,8,128]{2,1,0:T(8,128)(2,1)}, bf16[192,8,128]{2,1,0:T(8,128)(2,1)}, bf16[192,8,128]{2,1,0:T(8,128)(2,1)}) custom-call(bf16[4,8,192,128]{3,2,1,0:T(8,128)(2,1)S(1)} %shard_map.84.heads_ref), custom_call_target="tpu_custom_call" | custom-call | bytes 3145728 | tf_op jit(solution)/shard_map/pallas_call | solution.py:462
Async XLA Ops:
  0.6 1.0 %copy-start = (bf16[192,8,128]{2,1,0:T(8,128)(2,1)S(1)}, bf16[192,8,128]{2,1,0:T(8,128)(2,1)}, u32[]{:S(2)}) copy-start(bf16[192,8,128]{2,1,0:T(8,128)(2,1)} %key_ref.1) | copy-start | bytes 1179652
  1.6 1.0 %copy-start.1 = (bf16[192,8,128]{2,1,0:T(8,128)(2,1)S(1)}, bf16[192,8,128]{2,1,0:T(8,128)(2,1)}, u32[]{:S(2)}) copy-start(bf16[192,8,128]{2,1,0:T(8,128)(2,1)} %query_ref.1) | copy-start | bytes 1179652
  2.6 1.0 %copy-start.2 = (bf16[192,8,128]{2,1,0:T(8,128)(2,1)S(1)}, bf16[192,8,128]{2,1,0:T(8,128)(2,1)}, u32[]{:S(2)}) copy-start(bf16[192,8,128]{2,1,0:T(8,128)(2,1)} %value_ref.1) | copy-start | bytes 1179652
  3.6 1.0 %copy-start.3 = (bf16[192,8,128]{2,1,0:T(8,128)(2,1)S(1)}, bf16[192,8,128]{2,1,0:T(8,128)(2,1)}, u32[]{:S(2)}) copy-start(bf16[192,8,128]{2,1,0:T(8,128)(2,1)} %grad_ref.1) | copy-start | bytes 1179652
  4.6 0.7 copy-start.4

commit v3 on v2

--- a/solution.py
+++ b/solution.py
@@ -138,6 +138,7 @@
 
 KEY, QUERY, VALUE, GRAD = 0, 1, 2, 3
 OUT, DQ, DK, DV = 0, 1, 2, 3
+VMEM_BYTES = 62 * 1024 * 1024 + 600 * 1024
 LOG2E = 1.4426950408889634
 
 
@@ -155,11 +156,13 @@
     grad_ref,
     doc_ref,
     out_ref,
+    more_ref,
     fetched,
     staged,
     wide,
     full,
     ready,
+    zeros,
     doc_col,
     key_t,
     value_t,
@@ -173,8 +176,14 @@
     out_send,
     out_recv,
     fetch_sem,
+    low_send,
+    more_send,
+    more_recv,
+    zero_sem,
 ):
     me = lax.axis_index("ctx")
+    lower = shards // 2
+    low = me < lower
     size = half * group
     blocks = 2 * shards // group
     head_size = full.shape[-1]
@@ -219,10 +228,26 @@
     def far_first(step):
         return lax.rem(step + shards // 2 - 2, shards - 1) + 1
 
+    def stays_low(kind, part, target):
+        if part == 1 or kind in (KEY, VALUE):
+            return None
+        return low & (target >= lower)
+
+    def unless(skip, act):
+        if skip is None:
+            act()
+        else:
+            pl.when(jnp.logical_not(skip))(act)
+
     def sent_in(kind, part):
         def one(step, carry):
-            left = staged.at[kind, lax.rem(me + far_first(step), shards), part_rows(part)]
-            pltpu.make_async_copy(left, left, in_send.at[kind, part, step]).wait()
+            target = lax.rem(me + far_first(step), shards)
+
+            def act():
+                left = staged.at[kind, target, part_rows(part)]
+                pltpu.make_async_copy(left, left, in_send.at[kind, part, step]).wait()
+
+            unless(stays_low(kind, part, target), act)
             return carry
 
         lax.fori_loop(1, shards, one, 0)
@@ -237,17 +262,46 @@
 
         def one(step, carry):
             target = lax.rem(me + far_first(step), shards)
-            pltpu.make_async_remote_copy(
-                src_ref=staged.at[kind, target, part_rows(part)],
-                dst_ref=full.at[kind, block_rows(where)],
-                send_sem=in_send.at[kind, part, step],
-                recv_sem=in_recv.at[kind, where],
-                device_id={"ctx": target},
-                device_id_type=pl.DeviceIdType.MESH,
+
+            def act():
+                pltpu.make_async_remote_copy(
+                    src_ref=staged.at[kind, target, part_rows(part)],
+                    dst_ref=full.at[kind, block_rows(where)],
+                    send_sem=in_send.at[kind, part, step],
+                    recv_sem=in_recv.at[kind, where],
+                    device_id={"ctx": target},
+                    device_id_type=pl.DeviceIdType.MESH,
+                ).start()
+
+            unless(stays_low(kind, part, target), act)
+            return carry
+
+        lax.fori_loop(1, shards, one, 0)
+
+    def send_low(kind):
+        where = 2 * shards + me
+
+        @pl.when(low)
+        def _():
+            pltpu.make_async_copy(
+                staged.at[kind, me + lower, part_rows(0)],
+                full.at[kind, block_rows(where)],
+                in_recv.at[kind, where],
             ).start()
-            return carry
-
-        lax.fori_loop(1, shards, one, 0)
+
+            def one(step, carry):
+                target = lax.rem(me + step, lower)
+                pltpu.make_async_remote_copy(
+                    src_ref=staged.at[kind, target + lower, part_rows(0)],
+                    dst_ref=full.at[kind, block_rows(where)],
+                    send_sem=low_send.at[kind, step],
+                    recv_sem=in_recv.at[kind, where],
+                    device_id={"ctx": target},
+                    device_id_type=pl.DeviceIdType.MESH,
+                ).start()
+                return carry
+
+            lax.fori_loop(1, lower, one, 0)
 
     def wait_in(kind, block):
         def one(index, carry):
@@ -257,27 +311,44 @@
 
         lax.fori_loop(block * group, (block + 1) * group, one, 0)
 
+    def send_piece(held, place, owner, send_sem, recv_sem):
+        @pl.when(owner == me)
+        def _():
+            pltpu.make_async_copy(held, place, recv_sem).start()
+
+        @pl.when(owner != me)
+        def _():
+            pltpu.make_async_remote_copy(
+                src_ref=held,
+                dst_ref=place,
+                send_sem=send_sem,
+                recv_sem=recv_sem,
+                device_id={"ctx": owner},
+                device_id_type=pl.DeviceIdType.MESH,
+            ).start()
+
     def send_out(kind, block):
         for index in range(block * group, (block + 1) * group):
             part = 0 if index < shards else 1
             owner = index if part == 0 else 2 * shards - 1 - index
-            held = ready.at[kind, pl.ds(index * half, half)]
-            place = out_ref.at[kind, me, part_rows(part)]
-
-            @pl.when(owner == me)
-            def _():
-                pltpu.make_async_copy(held, place, out_recv.at[kind, part, me]).start()
-
-            @pl.when(owner != me)
-            def _():
-                pltpu.make_async_remote_copy(
-                    src_ref=held,
-                    dst_ref=place,
-                    send_sem=out_send.at[kind, index],
-                    recv_sem=out_recv.at[kind, part, me],
-                    device_id={"ctx": owner},
-                    device_id_type=pl.DeviceIdType.MESH,
-                ).start()
+            send_piece(
+                ready.at[kind, pl.ds(index * half, half)],
+                out_ref.at[kind, me, part_rows(part)],
+                owner,
+                out_send.at[kind, index],
+                out_recv.at[kind, part, me],
+            )
+
+    def send_more(kind):
+        for index in range(lower):
+            held = ready.at[kind, pl.ds((2 * shards + index) * half, half)]
+            if kind in (OUT, DQ):
+                place = out_ref.at[kind, me + lower, part_rows(0)]
+                recv_sem = out_recv.at[kind, 0, me + lower]
+            else:
+                place = more_ref.at[kind - DK, me]
+                recv_sem = more_recv.at[kind - DK, me]
+            send_piece(held, place, index, more_send.at[kind, index], recv_sem)
 
     stage(KEY)
     pl.semaphore_wait(barrier, shards - 1)
@@ -286,6 +357,8 @@
     send_in(QUERY, 0)
     stage(VALUE)
     send_in(VALUE, 0)
+    for kind in (KEY, QUERY, VALUE):
+        send_low(kind)
     stage(GRAD)
 
     docs = doc_ref[...].astype(jnp.float32).reshape(1, -1)
@@ -300,55 +373,66 @@
     def rows_of(block):
         return pl.ds(block * size, size)
 
-    for block in range(blocks):
-        if block == blocks // 2:
-            for kind, part in ((KEY, 1), (QUERY, 0)):
-                sent_in(kind, 1)
-                send_in(GRAD, part)
+    def turn_keys(block):
+        value_t[block] = full[VALUE, rows_of(block)].astype(jnp.float32).T.astype(jnp.bfloat16)
+        key_t[block] = full[KEY, rows_of(block)].astype(jnp.float32).T.astype(jnp.bfloat16)
+
+    def send_block(kind, block):
+        if block == blocks:
+            send_more(kind)
+        else:
+            send_out(kind, block)
+
+    def keys_of(block):
+        return [block] if block == blocks else list(reversed(range(block + 1)))
+
+    def forward(block):
+        keys = keys_of(block)
         wait_in(KEY, block)
         wait_in(QUERY, block)
         queries = full[QUERY, rows_of(block)]
-        query_doc = docs[:, block * size : (block + 1) * size]
+        at = block % blocks * size
+        query_doc = docs[:, at : at + size]
         largest = None
-        for other in range(block + 1):
+        for other in keys:
             scores = nt_dot(full[KEY, rows_of(other)], queries)
-            key_doc = jnp.concatenate([doc_col[other]] * (size // 128), axis=1)
+            key_doc = jnp.concatenate([doc_col[other % blocks]] * (size // 128), axis=1)
             seen = key_doc == query_doc
             if other == block:
                 key_at = lax.broadcasted_iota(jnp.int32, (size, size), 0)
                 query_at = lax.broadcasted_iota(jnp.int32, (size, size), 1)
                 seen = seen & (key_at <= query_at)
             scores = jnp.where(seen, scores, -1e30)
-            score_buf[other] = scores
+            score_buf[other % blocks] = scores
             top = jnp.max(scores, axis=0, keepdims=True)
             largest = top if largest is None else jnp.maximum(largest, top)
         total = jnp.zeros((1, size), jnp.float32)
-        for other in range(block + 1):
-            weights = jnp.exp2((score_buf[other] - largest) * (scaling * LOG2E))
-            score_buf[other] = weights
+        for other in keys:
+            weights = jnp.exp2((score_buf[other % blocks] - largest) * (scaling * LOG2E))
+            score_buf[other % blocks] = weights
             total = total + jnp.sum(weights, axis=0, keepdims=True)
         inverse = 1.0 / total
         wait_in(VALUE, block)
-        value_t[block] = full[VALUE, rows_of(block)].astype(jnp.float32).T.astype(jnp.bfloat16)
-        key_t[block] = full[KEY, rows_of(block)].astype(jnp.float32).T.astype(jnp.bfloat16)
+        turn_keys(block)
         accum = jnp.zeros((head_size, size), jnp.float32)
-        for other in range(block + 1):
-            probs = (score_buf[other] * inverse).astype(jnp.bfloat16)
-            prob_buf[block, other] = probs
+        for other in keys:
+            probs = (score_buf[other % blocks] * inverse).astype(jnp.bfloat16)
+            prob_buf[block, other % blocks] = probs
             accum = accum + jnp.dot(value_t[other], probs, preferred_element_type=jnp.float32)
         rounded = accum.astype(jnp.bfloat16).astype(jnp.float32)
         out_t[block] = rounded
         ready[OUT, rows_of(block)] = rounded.T.astype(jnp.bfloat16)
-        send_out(OUT, block)
-
-    for block in reversed(range(blocks)):
+        send_block(OUT, block)
+
+    def backward(block):
+        keys = keys_of(block)
         wait_in(GRAD, block)
         queries = full[QUERY, rows_of(block)]
         grads = full[GRAD, rows_of(block)]
         delta = jnp.sum(grads.astype(jnp.float32).T * out_t[block], axis=0, keepdims=True)
         accum = jnp.zeros((head_size, size), jnp.float32)
-        for other in range(block + 1):
-            probs = prob_buf[block, other]
+        for other in keys:
+            probs = prob_buf[block, other % blocks]
             dprobs = nt_dot(full[VALUE, rows_of(other)], grads)
             dscores = (probs.astype(jnp.float32) * (dprobs - delta)).astype(jnp.bfloat16)
             value_part = jnp.dot(probs, grads, preferred_element_type=jnp.float32)
@@ -360,15 +444,86 @@
                 value_acc[other] = value_part
                 key_acc[other] = key_part
             else:
-                ready[DV, rows_of(block)] = value_part.astype(jnp.bfloat16)
-                ready[DK, rows_of(block)] = (scaling * key_part).astype(jnp.bfloat16)
+                finish_keys(block, value_part, key_part)
             accum = accum + jnp.dot(key_t[other], dscores, preferred_element_type=jnp.float32)
         ready[DQ, rows_of(block)] = (scaling * accum).T.astype(jnp.bfloat16)
-        for kind in (DV, DK, DQ):
-            send_out(kind, block)
+        send_block(DQ, block)
+
+    def finish_keys(block, value_part, key_part):
+        ready[DV, rows_of(block)] = value_part.astype(jnp.bfloat16)
+        send_block(DV, block)
+        ready[DK, rows_of(block)] = (scaling * key_part).astype(jnp.bfloat16)
+        send_block(DK, block)
+
+    @pl.when(low)
+    def _():
+        forward(0)
+
+    @pl.when(jnp.logical_not(low))
+    def _():
+        zeros[...] = jnp.zeros_like(zeros)
+        pltpu.make_async_copy(zeros, more_ref, zero_sem).start()
+        wait_in(KEY, 0)
+        wait_in(VALUE, 0)
+        turn_keys(0)
+
+    for block in range(1, blocks):
+        if block == blocks // 2:
+            for kind, part in ((KEY, 1), (QUERY, 0)):
+                sent_in(kind, 1)
+                send_in(GRAD, part)
+            send_low(GRAD)
+
+            @pl.when(low)
+            def _():
+                forward(blocks)
+
+        forward(block)
+
+    for block in reversed(range(1, blocks)):
+        backward(block)
+
+    @pl.when(low)
+    def _():
+        backward(0)
+        backward(blocks)
+
+    @pl.when(jnp.logical_not(low))
+    def _():
+        finish_keys(0, value_acc[0], key_acc[0])
+        pltpu.make_async_copy(zeros, more_ref, zero_sem).wait()
 
     for kind, part in ((VALUE, 1), (GRAD, 1), (GRAD, 0)):
         sent_in(kind, part)
+
+    @pl.when(low)
+    def _():
+        def drain_low(step, carry):
+            for kind in range(4):
+                left = staged.at[kind, lax.rem(me + step, lower) + lower, part_rows(0)]
+                pltpu.make_async_copy(left, left, low_send.at[kind, step]).wait()
+            return carry
+
+        lax.fori_loop(1, lower, drain_low, 0)
+
+        def drain_more(index, carry):
+            @pl.when(index != me)
+            def _():
+                for kind in range(4):
+                    left = ready.at[kind, block_rows(2 * shards + index)]
+                    pltpu.make_async_copy(left, left, more_send.at[kind, index]).wait()
+
+            return carry
+
+        lax.fori_loop(0, lower, drain_more, 0)
+
+        def collect_more(source, carry):
+            for kind in range(2):
+                place = more_ref.at[kind, source]
+                pltpu.make_async_copy(place, place, more_recv.at[kind, source]).wait()
+            return carry
+
+        lax.fori_loop(0, lower, collect_more, 0)
 
     def drain_out(index, carry):
         owner = jnp.where(index < shards, index, 2 * shards - 1 - index)
@@ -376,8 +531,13 @@
         @pl.when(owner != me)
         def _():
             for kind in range(4):
-                left = ready.at[kind, block_rows(index)]
-                pltpu.make_async_copy(left, left, out_send.at[kind, index]).wait()
+
+                def act():
+                    left = ready.at[kind, block_rows(index)]
+                    pltpu.make_async_copy(left, left, out_send.at[kind, index]).wait()
+
+                kept = jnp.logical_not(low) & (index < lower) if kind in (OUT, DQ) else None
+                unless(kept, act)
 
         return carry
 
@@ -393,7 +553,9 @@
     lax.fori_loop(0, shards, collect, 0)
 
 
-def rows_kernel(heads_ref, out_a, out_b, out_c, out_d, held, wide, turned, in_sem, out_sem):
+def rows_kernel(
+    heads_ref, more_ref, out_a, out_b, out_c, out_d, held, more, wide, turned, in_sem, out_sem
+):
     heads, rows, head_size = held.shape[1:]
     outs = (out_a, out_b, out_c, out_d)
     reads = [
@@ -403,12 +565,21 @@
     writes = [
         pltpu.make_async_copy(turned.at[kind], outs[kind], out_sem.at[kind]) for kind in range(4)
     ]
+    lower, half = more.shape[1:3]
+    late = pltpu.make_async_copy(more_ref, more, in_sem.at[4])
+    late.start()
     for read in reads:
         read.start()
     for kind in range(4):
         reads[kind].wait()
+        if kind == DK:
+            late.wait()
         for head in range(heads):
             wide[pl.ds(head, rows, stride=heads), :] = held[kind, head].astype(jnp.float32)
+        if kind in (DK, DV):
+            for head in range(lower, heads):
+                first = pl.ds(head, half, stride=heads)
+                wide[first, :] = wide[first, :] + more[kind - DK, head - lower].astype(jnp.float32)
         turned[kind] = wide[...].reshape(rows, heads, head_size).astype(jnp.bfloat16)
         writes[kind].start()
     for write in writes:
@@ -426,33 +597,41 @@
     bf16, f32 = jnp.bfloat16, jnp.float32
     vmem = pl.BlockSpec(memory_space=pltpu.VMEM)
     flops = 7 * tokens * tokens * head_size
-    results = pl.pallas_call(
+    results, more = pl.pallas_call(
         functools.partial(head_kernel, shards, half, group),
-        out_shape=jax.ShapeDtypeStruct((4, shards, shard_rows, head_size), bf16),
+        out_shape=[
+            jax.ShapeDtypeStruct((4, shards, shard_rows, head_size), bf16),
+            jax.ShapeDtypeStruct((2, shards // 2, half, head_size), bf16),
+        ],
         in_specs=[pl.BlockSpec(memory_space=pltpu.HBM)] * 4 + [vmem],
-        out_specs=pl.BlockSpec(memory_space=pl.ANY),
+        out_specs=[pl.BlockSpec(memory_space=pl.ANY)] * 2,
         scratch_shapes=[
             pltpu.VMEM((4, shard_rows, shards, head_size), bf16),
             pltpu.VMEM((4, shards, shard_rows, head_size), bf16),
             pltpu.VMEM((tokens, head_size), f32),
-            pltpu.VMEM((4, tokens, head_size), bf16),
-            pltpu.VMEM((4, tokens, head_size), bf16),
+            pltpu.VMEM((4, tokens + size, head_size), bf16),
+            pltpu.VMEM((4, tokens + size, head_size), bf16),
+            pltpu.VMEM((2, shards // 2, half, head_size), bf16),
             pltpu.VMEM((blocks, size, 128), f32),
-            pltpu.VMEM((blocks, head_size, size), bf16),
-            pltpu.VMEM((blocks, head_size, size), bf16),
-            pltpu.VMEM((blocks, head_size, size), f32),
+            pltpu.VMEM((blocks + 1, head_size, size), bf16),
+            pltpu.VMEM((blocks + 1, head_size, size), bf16),
+            pltpu.VMEM((blocks + 1, head_size, size), f32),
             pltpu.VMEM((blocks, size, size), f32),
-            pltpu.VMEM((blocks, blocks, size, size), bf16),
+            pltpu.VMEM((blocks + 1, blocks, size, size), bf16),
             pltpu.VMEM((blocks, size, head_size), f32),
             pltpu.VMEM((blocks, size, head_size), f32),
             pltpu.SemaphoreType.DMA((4, 2, shards)),
-            pltpu.SemaphoreType.DMA((4, 2 * shards)),
+            pltpu.SemaphoreType.DMA((4, 2 * shards + shards // 2)),
             pltpu.SemaphoreType.DMA((4, 2 * shards)),
             pltpu.SemaphoreType.DMA((4, 2, shards)),
             pltpu.SemaphoreType.DMA((4,)),
+            pltpu.SemaphoreType.DMA((4, shards // 2)),
+            pltpu.SemaphoreType.DMA((4, shards // 2)),
+            pltpu.SemaphoreType.DMA((2, shards // 2)),
+            pltpu.SemaphoreType.DMA,
         ],
         compiler_params=pltpu.CompilerParams(
-            collective_id=0, has_side_effects=True, vmem_limit_bytes=40 * 1024 * 1024
+            collective_id=0, has_side_effects=True, vmem_limit_bytes=VMEM_BYTES
         ),
         cost_estimate=pl.CostEstimate(
             flops=flops, bytes_accessed=8 * queries.size * 2, transcendentals=tokens * tokens // 2
@@ -462,26 +641,28 @@
     return pl.pallas_call(
         rows_kernel,
         out_shape=[rows_first] * 4,
-        in_specs=[pl.BlockSpec(memory_space=pl.ANY)],
+        in_specs=[pl.BlockSpec(memory_space=pl.ANY)] * 2,
         out_specs=[pl.BlockSpec(memory_space=pl.ANY)] * 4,
         scratch_shapes=[
             pltpu.VMEM((4, shards, shard_rows, head_size), bf16),
+            pltpu.VMEM((2, shards // 2, half, head_size), bf16),
             pltpu.VMEM((shard_rows * shards, head_size), f32),
             pltpu.VMEM((4, shard_rows, shards, head_size), bf16),
-            pltpu.SemaphoreType.DMA((4,)),
+            pltpu.SemaphoreType.DMA((5,)),
             pltpu.SemaphoreType.DMA((4,)),
         ],
         compiler_params=pltpu.CompilerParams(vmem_limit_bytes=16 * 1024 * 1024),
         cost_estimate=pl.CostEstimate(
             flops=0, bytes_accessed=16 * queries.size, transcendentals=0
         ),
-    )(results)
+    )(results, more)
 
 
 def on_device(queries, key_vecs, value_vecs, out_grad, doc_ids):
     shard_rows, head_count, head_size = queries.shape
     fits = (
         head_count == lax.axis_size("ctx")
+        and head_count == 8
         and shard_rows % 32 == 0
         and (2 * shard_rows) % 128 == 0
         and head_size == 128

time: 84.8 us -> 80.1 us (0.945)
  the two profiles are of different devices: /device:TPU:0 before, /device:TPU:28 now
where the time goes in v3:
time: 80.1 us; the launch traced here: 79.8 us
  Pallas kernels  76.9 us (96%)
  local copies, waits for them, and re-layouts  2.33 us (3%)
    pallas_call x1, Pallas kernels, by_heads(): pl.pallas_call(functools.partial(head_kernel, shards, half, group), out_s...  74 us
    pallas_call x1, Pallas kernels, by_heads(): pl.pallas_call(rows_kernel, out_shape=[rows_first] * 4, in_specs=[pl.Bloc...  2.86 us
    unnamed x4, local copies, waits for them, and re-layouts  2.33 us

profile of v3, /device:TPU:28, one launch (start us, length us, event | category | flops | bytes accessed | tf_op | source)
XLA Modules:
  0.0 79.8 jit_solution(2823659209938493100)
XLA Ops:
  0.6 74.0 %shard_map.84 = (bf16[4,8,192,128]{3,2,1,0:T(8,128)(2,1)}, bf16[2,4,96,128]{3,2,1,0:T(8,128)(2,1)}) custom-call(bf16[192,8,128]{2,1,0:T(8,128)(2,1)} %key_ref.1, bf16[192,8,128]{2,1,0:T(8,128)(2,1)} %query_ref.1, bf16[192,8,128]{2,1,0:T(8,128)(2,1)} %value_ref.1, bf16[192,8,128]{2,1,0:T(8,128)(2,1)} %grad_ref.1, s32[1536]{0:T(1024)} %doc_ref.1), custom_call_target="tpu_custom_call" | custom-call | flops 2113929216 | bytes 3145728 | tf_op jit(solution)/shard_map/pallas_call | solution.py:600
  74.6 0.0 copy-start
  74.6 1.4 %copy-done = bf16[4,8,192,128]{3,2,1,0:T(8,128)(2,1)S(1)} copy-done((bf16[4,8,192,128]{3,2,1,0:T(8,128)(2,1)S(1)}, bf16[4,8,192,128]{3,2,1,0:T(8,128)(2,1)}, u32[]{:S(2)}) %copy-start) | copy-done | bytes 1572888
  76.0 0.0 copy-start.1
  76.0 0.9 %copy-done.1 = bf16[2,4,96,128]{3,2,1,0:T(8,128)(2,1)S(1)} copy-done((bf16[2,4,96,128]{3,2,1,0:T(8,128)(2,1)S(1)}, bf16[2,4,96,128]{3,2,1,0:T(8,128)(2,1)}, u32[]{:S(2)}) %copy-start.1) | copy-done | bytes 196632
  77.0 2.9 %shard_map.85 = (bf16[192,8,128]{2,1,0:T(8,128)(2,1)}, bf16[192,8,128]{2,1,0:T(8,128)(2,1)}, bf16[192,8,128]{2,1,0:T(8,128)(2,1)}, bf16[192,8,128]{2,1,0:T(8,128)(2,1)}) custom-call(bf16[4,8,192,128]{3,2,1,0:T(8,128)(2,1)S(1)} %copy-done, bf16[2,4,96,128]{3,2,1,0:T(8,128)(2,1)S(1)} %copy-done.1), custom_call_target="tpu_custom_call" | custom-call | bytes 3145728 | tf_op jit(solution)/shard_map/pallas_call | solution.py:641
Async XLA Ops:
  74.6 1.4 %copy-start = (bf16[4,8,192,128]{3,2,1,0:T(8,128)(2,1)S(1)}, bf16[4,8,192,128]{3,2,1,0:T(8,128)(2,1)}, u32[]{:S(2)}) copy-start(bf16[4,8,192,128]{3,2,1,0:T(8,128)(2,1)} %get-tuple-element.6.heads_ref) | copy-start | bytes 4718596
  76.0 0.9 %copy-start.1 = (bf16[2,4,96,128]{3,2,1,0:T(8,128)(2,1)S(1)}, bf16[2,4,96,128]{3,2,1,0:T(8,128)(2,1)}, u32[]{:S(2)}) copy-start(bf16[2,4,96,128]{3,2,1,0:T(8,128)(2,1)} %get-tuple-element.7.more_ref) | copy-start | bytes 589828

commit v4 on v3

--- a/solution.py
+++ b/solution.py
@@ -179,11 +179,15 @@
     low_send,
     more_send,
     more_recv,
+    help_send,
     zero_sem,
 ):
     me = lax.axis_index("ctx")
     lower = shards // 2
     low = me < lower
+    helpers = lower // 2
+    helped = me < helpers
+    helping = (me >= lower) & (me < lower + helpers)
     size = half * group
     blocks = 2 * shards // group
     head_size = full.shape[-1]
@@ -228,10 +232,10 @@
     def far_first(step):
         return lax.rem(step + shards // 2 - 2, shards - 1) + 1
 
-    def stays_low(kind, part, target):
+    def diverted(kind, part, target):
         if part == 1 or kind in (KEY, VALUE):
             return None
-        return low & (target >= lower)
+        return (low & (target >= lower)) | ((me >= lower) & (target < helpers))
 
     def unless(skip, act):
         if skip is None:
@@ -247,7 +251,7 @@
                 left = staged.at[kind, target, part_rows(part)]
                 pltpu.make_async_copy(left, left, in_send.at[kind, part, step]).wait()
 
-            unless(stays_low(kind, part, target), act)
+            unless(diverted(kind, part, target), act)
             return carry
 
         lax.fori_loop(1, shards, one, 0)
@@ -273,7 +277,7 @@
                     device_id_type=pl.DeviceIdType.MESH,
                 ).start()
 
-            unless(stays_low(kind, part, target), act)
+            unless(diverted(kind, part, target), act)
             return carry
 
         lax.fori_loop(1, shards, one, 0)
@@ -303,6 +307,17 @@
 
             lax.fori_loop(1, lower, one, 0)
 
+        for head in range(helpers):
+            held = staged.at[kind, head, part_rows(0)]
+            place = full.at[kind, block_rows(where)]
+
+            def act():
+                send_piece(
+                    held, place, lower + head, help_send.at[kind, head], in_recv.at[kind, where]
+                )
+
+            unless(low if kind in (QUERY, GRAD) else None, act)
+
     def wait_in(kind, block):
         def one(index, carry):
             held = full.at[kind, block_rows(index)]
@@ -339,16 +354,17 @@
                 out_recv.at[kind, part, me],
             )
 
-    def send_more(kind):
-        for index in range(lower):
-            held = ready.at[kind, pl.ds((2 * shards + index) * half, half)]
+    def send_more(kind, block, head):
+        for step in range(group):
+            owner = (block - blocks) * group + step
+            held = ready.at[kind, pl.ds((2 * shards + owner) * half, half)]
             if kind in (OUT, DQ):
-                place = out_ref.at[kind, me + lower, part_rows(0)]
-                recv_sem = out_recv.at[kind, 0, me + lower]
+                place = out_ref.at[kind, head, part_rows(0)]
+                recv_sem = out_recv.at[kind, 0, head]
             else:
                 place = more_ref.at[kind - DK, me]
                 recv_sem = more_recv.at[kind - DK, me]
-            send_piece(held, place, index, more_send.at[kind, index], recv_sem)
+            send_piece(held, place, owner, more_send.at[kind, owner], recv_sem)
 
     stage(KEY)
     pl.semaphore_wait(barrier, shards - 1)
@@ -377,17 +393,22 @@
         value_t[block] = full[VALUE, rows_of(block)].astype(jnp.float32).T.astype(jnp.bfloat16)
         key_t[block] = full[KEY, rows_of(block)].astype(jnp.float32).T.astype(jnp.bfloat16)
 
-    def send_block(kind, block):
-        if block == blocks:
-            send_more(kind)
+    def send_block(kind, block, head):
+        if block >= blocks:
+            send_more(kind, block, head)
         else:
             send_out(kind, block)
 
     def keys_of(block):
-        return [block] if block == blocks else list(reversed(range(block + 1)))
-
-    def forward(block):
+        return list(range(block, blocks - 1 if block >= blocks else -1, -1))
+
+    def forward(block, head=None):
         keys = keys_of(block)
+        for other in keys[1:]:
+            if block >= blocks:
+                wait_in(KEY, other)
+                wait_in(VALUE, other)
+                turn_keys(other)
         wait_in(KEY, block)
         wait_in(QUERY, block)
         queries = full[QUERY, rows_of(block)]
@@ -422,9 +443,9 @@
         rounded = accum.astype(jnp.bfloat16).astype(jnp.float32)
         out_t[block] = rounded
         ready[OUT, rows_of(block)] = rounded.T.astype(jnp.bfloat16)
-        send_block(OUT, block)
-
-    def backward(block):
+        send_block(OUT, block, head)
+
+    def backward(block, head=None):
         keys = keys_of(block)
         wait_in(GRAD, block)
         queries = full[QUERY, rows_of(block)]
@@ -440,58 +461,62 @@
             if block < blocks - 1:
                 value_part = value_part + value_acc[other]
                 key_part = key_part + key_acc[other]
-            if other < block:
+            if block >= blocks:
+                finish_keys(other, value_part, key_part, head)
+            elif other < block:
                 value_acc[other] = value_part
                 key_acc[other] = key_part
             else:
-                finish_keys(block, value_part, key_part)
+                finish_keys(block, value_part, key_part, head)
             accum = accum + jnp.dot(key_t[other], dscores, preferred_element_type=jnp.float32)
         ready[DQ, rows_of(block)] = (scaling * accum).T.astype(jnp.bfloat16)
-        send_block(DQ, block)
-
-    def finish_keys(block, value_part, key_part):
+        send_block(DQ, block, head)
+
+    def finish_keys(block, value_part, key_part, head=None):
         ready[DV, rows_of(block)] = value_part.astype(jnp.bfloat16)
-        send_block(DV, block)
+        send_block(DV, block, head)
         ready[DK, rows_of(block)] = (scaling * key_part).astype(jnp.bfloat16)
-        send_block(DK, block)
-
-    @pl.when(low)
-    def _():
-        forward(0)
-
-    @pl.when(jnp.logical_not(low))
-    def _():
+        send_block(DK, block, head)
+
+    def keys_alone(block):
+        wait_in(KEY, block)
+        wait_in(VALUE, block)
+        turn_keys(block)
+
+    def either(condition, first, second):
+        pl.when(condition)(first)
+        pl.when(jnp.logical_not(condition))(second)
+
+    spare = more_ref.at[:, pl.ds(0, lower)]
+
+    def fill_zeros():
         zeros[...] = jnp.zeros_like(zeros)
-        pltpu.make_async_copy(zeros, more_ref, zero_sem).start()
-        wait_in(KEY, 0)
-        wait_in(VALUE, 0)
-        turn_keys(0)
-
-    for block in range(1, blocks):
-        if block == blocks // 2:
-            for kind, part in ((KEY, 1), (QUERY, 0)):
-                sent_in(kind, 1)
-                send_in(GRAD, part)
-            send_low(GRAD)
-
-            @pl.when(low)
-            def _():
-                forward(blocks)
-
+        pltpu.make_async_copy(zeros, spare, zero_sem).start()
+        keys_alone(0)
+
+    either(low, lambda: forward(0), fill_zeros)
+    either(helped, lambda: keys_alone(1), lambda: forward(1))
+    for kind, part in ((KEY, 1), (QUERY, 0)):
+        sent_in(kind, 1)
+        send_in(GRAD, part)
+    send_low(GRAD)
+    pl.when(low)(lambda: forward(blocks, me + lower))
+    pl.when(helping)(lambda: forward(blocks + 1, me - lower))
+    for block in range(2, blocks):
         forward(block)
 
-    for block in reversed(range(1, blocks)):
+    for block in reversed(range(2, blocks)):
         backward(block)
 
-    @pl.when(low)
-    def _():
-        backward(0)
-        backward(blocks)
-
-    @pl.when(jnp.logical_not(low))
-    def _():
+    either(helped, lambda: finish_keys(1, value_acc[1], key_acc[1]), lambda: backward(1))
+
+    def upper_end():
         finish_keys(0, value_acc[0], key_acc[0])
-        pltpu.make_async_copy(zeros, more_ref, zero_sem).wait()
+        pltpu.make_async_copy(zeros, spare, zero_sem).wait()
+
+    either(low, lambda: backward(0), upper_end)
+    pl.when(low)(lambda: backward(blocks, me + lower))
+    pl.when(helping)(lambda: backward(blocks + 1, me - lower))
 
     for kind, part in ((VALUE, 1), (GRAD, 1), (GRAD, 0)):
         sent_in(kind, part)
@@ -517,13 +542,46 @@
 
         lax.fori_loop(0, lower, drain_more, 0)
 
-        def collect_more(source, carry):
-            for kind in range(2):
-                place = more_ref.at[kind, source]
-                pltpu.make_async_copy(place, place, more_recv.at[kind, source]).wait()
+    @pl.when(helping)
+    def _():
+        def drain_more(index, carry):
+            @pl.when(index != me)
+            def _():
+                for kind in range(4):
+
+                    def act():
+                        left = ready.at[kind, block_rows(2 * shards + index)]
+                        pltpu.make_async_copy(left, left, more_send.at[kind, index]).wait()
+
+                    unless(index < lower if kind in (OUT, DQ) else None, act)
+
             return carry
 
+        lax.fori_loop(0, shards, drain_more, 0)
+
+    for head in range(helpers):
+
+        @pl.when(me != lower + head)
+        def _():
+            for kind in range(4):
+
+                def act():
+                    left = staged.at[kind, head, part_rows(0)]
+                    pltpu.make_async_copy(left, left, help_send.at[kind, head]).wait()
+
+                unless(low if kind in (QUERY, GRAD) else None, act)
+
+    def collect_more(source, carry):
+        for kind in range(2):
+            place = more_ref.at[kind, source]
+            pltpu.make_async_copy(place, place, more_recv.at[kind, source]).wait()
+        return carry
+
+    @pl.when(low)
+    def _():
         lax.fori_loop(0, lower, collect_more, 0)
+
+    lax.fori_loop(lower, lower + helpers, collect_more, 0)
 
     def drain_out(index, carry):
         owner = jnp.where(index < shards, index, 2 * shards - 1 - index)
@@ -536,7 +594,11 @@
                     left = ready.at[kind, block_rows(index)]
                     pltpu.make_async_copy(left, left, out_send.at[kind, index]).wait()
 
-                kept = jnp.logical_not(low) & (index < lower) if kind in (OUT, DQ) else None
+                kept = None
+                if kind in (OUT, DQ):
+                    kept = (jnp.logical_not(low) & (index < lower)) | (
+                        helped & (index >= lower) & (index < shards)
+                    )
                 unless(kept, act)
 
         return carry
@@ -565,7 +627,7 @@
     writes = [
         pltpu.make_async_copy(turned.at[kind], outs[kind], out_sem.at[kind]) for kind in range(4)
     ]
-    lower, half = more.shape[1:3]
+    half = more.shape[2]
     late = pltpu.make_async_copy(more_ref, more, in_sem.at[4])
     late.start()
     for read in reads:
@@ -577,9 +639,9 @@
         for head in range(heads):
             wide[pl.ds(head, rows, stride=heads), :] = held[kind, head].astype(jnp.float32)
         if kind in (DK, DV):
-            for head in range(lower, heads):
-                first = pl.ds(head, half, stride=heads)
-                wide[first, :] = wide[first, :] + more[kind - DK, head - lower].astype(jnp.float32)
+            for slot in range(more.shape[1]):
+                first = pl.ds((slot + heads // 2) % heads, half, stride=heads)
+                wide[first, :] = wide[first, :] + more[kind - DK, slot].astype(jnp.float32)
         turned[kind] = wide[...].reshape(rows, heads, head_size).astype(jnp.bfloat16)
         writes[kind].start()
     for write in writes:
@@ -594,6 +656,7 @@
     group = 4
     size = group * half
     blocks = tokens // size
+    slots = shards // 2 + shards // 4
     bf16, f32 = jnp.bfloat16, jnp.float32
     vmem = pl.BlockSpec(memory_space=pltpu.VMEM)
     flops = 7 * tokens * tokens * head_size
@@ -601,7 +664,7 @@
         functools.partial(head_kernel, shards, half, group),
         out_shape=[
             jax.ShapeDtypeStruct((4, shards, shard_rows, head_size), bf16),
-            jax.ShapeDtypeStruct((2, shards // 2, half, head_size), bf16),
+            jax.ShapeDtypeStruct((2, slots, half, head_size), bf16),
         ],
         in_specs=[pl.BlockSpec(memory_space=pltpu.HBM)] * 4 + [vmem],
         out_specs=[pl.BlockSpec(memory_space=pl.ANY)] * 2,
@@ -609,25 +672,26 @@
             pltpu.VMEM((4, shard_rows, shards, head_size), bf16),
             pltpu.VMEM((4, shards, shard_rows, head_size), bf16),
             pltpu.VMEM((tokens, head_size), f32),
-            pltpu.VMEM((4, tokens + size, head_size), bf16),
-            pltpu.VMEM((4, tokens + size, head_size), bf16),
+            pltpu.VMEM((4, tokens + 2 * size, head_size), bf16),
+            pltpu.VMEM((4, tokens + 2 * size, head_size), bf16),
             pltpu.VMEM((2, shards // 2, half, head_size), bf16),
             pltpu.VMEM((blocks, size, 128), f32),
-            pltpu.VMEM((blocks + 1, head_size, size), bf16),
-            pltpu.VMEM((blocks + 1, head_size, size), bf16),
-            pltpu.VMEM((blocks + 1, head_size, size), f32),
+            pltpu.VMEM((blocks + 2, head_size, size), bf16),
+            pltpu.VMEM((blocks + 2, head_size, size), bf16),
+            pltpu.VMEM((blocks + 2, head_size, size), f32),
             pltpu.VMEM((blocks, size, size), f32),
-            pltpu.VMEM((blocks + 1, blocks, size, size), bf16),
+            pltpu.VMEM((blocks + 2, blocks, size, size), bf16),
             pltpu.VMEM((blocks, size, head_size), f32),
             pltpu.VMEM((blocks, size, head_size), f32),
             pltpu.SemaphoreType.DMA((4, 2, shards)),
-            pltpu.SemaphoreType.DMA((4, 2 * shards + shards // 2)),
+            pltpu.SemaphoreType.DMA((4, 3 * shards)),
             pltpu.SemaphoreType.DMA((4, 2 * shards)),
             pltpu.SemaphoreType.DMA((4, 2, shards)),
             pltpu.SemaphoreType.DMA((4,)),
             pltpu.SemaphoreType.DMA((4, shards // 2)),
-            pltpu.SemaphoreType.DMA((4, shards // 2)),
-            pltpu.SemaphoreType.DMA((2, shards // 2)),
+            pltpu.SemaphoreType.DMA((4, shards)),
+            pltpu.SemaphoreType.DMA((2, slots)),
+            pltpu.SemaphoreType.DMA((4, shards // 4)),
             pltpu.SemaphoreType.DMA,
         ],
         compiler_params=pltpu.CompilerParams(
@@ -645,13 +709,13 @@
         out_specs=[pl.BlockSpec(memory_space=pl.ANY)] * 4,
         scratch_shapes=[
             pltpu.VMEM((4, shards, shard_rows, head_size), bf16),
-            pltpu.VMEM((2, shards // 2, half, head_size), bf16),
+            pltpu.VMEM((2, slots, half, head_size), bf16),
             pltpu.VMEM((shard_rows * shards, head_size), f32),
             pltpu.VMEM((4, shard_rows, shards, head_size), bf16),
             pltpu.SemaphoreType.DMA((5,)),
             pltpu.SemaphoreType.DMA((4,)),
         ],
-        compiler_params=pltpu.CompilerParams(vmem_limit_bytes=16 * 1024 * 1024),
+        compiler_params=pltpu.CompilerParams(vmem_limit_bytes=VMEM_BYTES),
         cost_estimate=pl.CostEstimate(
             flops=0, bytes_accessed=16 * queries.size, transcendentals=0
         ),

time: 80.1 us -> 74.9 us (0.935)
  the two profiles are of different devices: /device:TPU:28 before, /device:TPU:0 now
where the time goes in v4:
time: 74.9 us; the launch traced here: 74.7 us
  Pallas kernels  73.9 us (99%)
  between operations  0.8 us (1%)
    pallas_call x1, Pallas kernels, by_heads(): pl.pallas_call(functools.partial(head_kernel, shards, half, group), out_s...  70.8 us
    pallas_call x1, Pallas kernels, by_heads(): pl.pallas_call(rows_kernel, out_shape=[rows_first] * 4, in_specs=[pl.Bloc...  3.05 us

profile of v4, /device:TPU:0, one launch (start us, length us, event | category | flops | bytes accessed | tf_op | source)
XLA Modules:
  0.0 74.7 jit_solution(18189802207592580626)
XLA Ops:
  0.6 70.8 %shard_map.84 = (bf16[4,8,192,128]{3,2,1,0:T(8,128)(2,1)}, bf16[2,6,96,128]{3,2,1,0:T(8,128)(2,1)}) custom-call(bf16[192,8,128]{2,1,0:T(8,128)(2,1)} %key_ref.1, bf16[192,8,128]{2,1,0:T(8,128)(2,1)} %query_ref.1, bf16[192,8,128]{2,1,0:T(8,128)(2,1)} %value_ref.1, bf16[192,8,128]{2,1,0:T(8,128)(2,1)} %grad_ref.1, s32[1536]{0:T(1024)} %doc_ref.1), custom_call_target="tpu_custom_call" | custom-call | flops 2113929216 | bytes 3145728 | tf_op jit(solution)/shard_map/pallas_call | solution.py:663
  71.5 3.0 %shard_map.85 = (bf16[192,8,128]{2,1,0:T(8,128)(2,1)}, bf16[192,8,128]{2,1,0:T(8,128)(2,1)}, bf16[192,8,128]{2,1,0:T(8,128)(2,1)}, bf16[192,8,128]{2,1,0:T(8,128)(2,1)}) custom-call(bf16[4,8,192,128]{3,2,1,0:T(8,128)(2,1)} %get-tuple-element.6.heads_ref, bf16[2,6,96,128]{3,2,1,0:T(8,128)(2,1)} %get-tuple-element.7.more_ref), custom_call_target="tpu_custom_call" | custom-call | bytes 3145728 | tf_op jit(solution)/shard_map/pallas_call | solution.py:705

commit v5 on v4

--- a/solution.py
+++ b/solution.py
@@ -171,6 +171,8 @@
     prob_buf,
     key_acc,
     value_acc,
+    query_acc,
+    deltas,
     in_send,
     in_recv,
     out_send,
@@ -445,32 +447,45 @@
         ready[OUT, rows_of(block)] = rounded.T.astype(jnp.bfloat16)
         send_block(OUT, block, head)
 
-    def backward(block, head=None):
-        keys = keys_of(block)
-        wait_in(GRAD, block)
-        queries = full[QUERY, rows_of(block)]
-        grads = full[GRAD, rows_of(block)]
-        delta = jnp.sum(grads.astype(jnp.float32).T * out_t[block], axis=0, keepdims=True)
-        accum = jnp.zeros((head_size, size), jnp.float32)
-        for other in keys:
+    def backward(pairs, new=(), done=(), head=None):
+        for block, other in pairs:
+            queries = full[QUERY, rows_of(block)]
+            grads = full[GRAD, rows_of(block)]
             probs = prob_buf[block, other % blocks]
             dprobs = nt_dot(full[VALUE, rows_of(other)], grads)
-            dscores = (probs.astype(jnp.float32) * (dprobs - delta)).astype(jnp.bfloat16)
+            dscores = (probs.astype(jnp.float32) * (dprobs - deltas[block])).astype(jnp.bfloat16)
             value_part = jnp.dot(probs, grads, preferred_element_type=jnp.float32)
             key_part = jnp.dot(dscores, queries, preferred_element_type=jnp.float32)
-            if block < blocks - 1:
+            query_part = jnp.dot(key_t[other], dscores, preferred_element_type=jnp.float32)
+            if ("k", block, other) not in new:
                 value_part = value_part + value_acc[other]
                 key_part = key_part + key_acc[other]
-            if block >= blocks:
+            if ("k", block, other) in done:
                 finish_keys(other, value_part, key_part, head)
-            elif other < block:
+            else:
                 value_acc[other] = value_part
                 key_acc[other] = key_part
+            if ("q", block, other) not in new:
+                query_part = query_part + query_acc[block]
+            if ("q", block, other) in done:
+                ready[DQ, rows_of(block)] = (scaling * query_part).T.astype(jnp.bfloat16)
+                send_block(DQ, block, head)
             else:
-                finish_keys(block, value_part, key_part, head)
-            accum = accum + jnp.dot(key_t[other], dscores, preferred_element_type=jnp.float32)
-        ready[DQ, rows_of(block)] = (scaling * accum).T.astype(jnp.bfloat16)
-        send_block(DQ, block, head)
+                query_acc[block] = query_part
+
+    def ready_grads(block):
+        wait_in(GRAD, block)
+        grads = full[GRAD, rows_of(block)].astype(jnp.float32)
+        deltas[block] = jnp.sum(grads.T * out_t[block], axis=0, keepdims=True)
+
+    def plan(pairs):
+        seen, new = set(), []
+        for block, other in pairs:
+            for name in (("q", block), ("k", other)):
+                if name not in seen:
+                    new.append((name[0], block, other))
+                seen.add(name)
+        return new
 
     def finish_keys(block, value_part, key_part, head=None):
         ready[DV, rows_of(block)] = value_part.astype(jnp.bfloat16)
@@ -505,18 +520,56 @@
     for block in range(2, blocks):
         forward(block)
 
-    for block in reversed(range(2, blocks)):
-        backward(block)
-
-    either(helped, lambda: finish_keys(1, value_acc[1], key_acc[1]), lambda: backward(1))
-
-    def upper_end():
-        finish_keys(0, value_acc[0], key_acc[0])
+    def lower_backward():
+        late = blocks - 1
+        first = [(late, 2), (2, 2), (2, 1), (2, 0), (late, 1)]
+        backward(first, plan(first), [("k", 2, 2), ("q", 2, 0)])
+
+        def second():
+            ready_grads(1)
+            backward(
+                [(1, 1), (1, 0)], [("q", 1, 1)], [("k", 1, 1), ("q", 1, 0)]
+            )
+
+        either(helped, lambda: finish_keys(1, value_acc[1], key_acc[1]), second)
+        home = [(late, 0), (late, late)]
+        backward(home, [("k", late, late)], [("k", late, late), ("q", late, late)])
+        ready_grads(0)
+        backward([(0, 0)], [("q", 0, 0)], [("k", 0, 0), ("q", 0, 0)])
+        extra = blocks
+        ready_grads(extra)
+        both = [("q", extra, extra), ("k", extra, extra)]
+        backward([(extra, extra)], both, both, me + lower)
+
+    def upper_backward():
+        late = blocks - 1
+        first = [(late, late), (late, 2), (late, 1), (late, 0), (2, 0)]
+        backward(first, plan(first), [("k", late, late), ("q", late, 0)])
+        ready_grads(1)
+        backward([(1, 0)], [("q", 1, 0)], [("k", 1, 0)])
+
+        @pl.when(helping)
+        def _():
+            extra = blocks + 1
+            ready_grads(extra)
+            pairs = [(extra, blocks), (extra, extra)]
+            backward(
+                pairs,
+                plan(pairs),
+                [("k", extra, blocks), ("k", extra, extra), ("q", extra, extra)],
+                me - lower,
+            )
+
+        backward(
+            [(2, 2), (2, 1), (1, 1)],
+            [],
+            [("k", 2, 2), ("q", 2, 1), ("k", 1, 1), ("q", 1, 1)],
+        )
         pltpu.make_async_copy(zeros, spare, zero_sem).wait()
 
-    either(low, lambda: backward(0), upper_end)
-    pl.when(low)(lambda: backward(blocks, me + lower))
-    pl.when(helping)(lambda: backward(blocks + 1, me - lower))
+    for block in range(2, blocks):
+        ready_grads(block)
+    either(low, lower_backward, upper_backward)
 
     for kind, part in ((VALUE, 1), (GRAD, 1), (GRAD, 0)):
         sent_in(kind, part)
@@ -681,8 +734,10 @@
             pltpu.VMEM((blocks + 2, head_size, size), f32),
             pltpu.VMEM((blocks, size, size), f32),
             pltpu.VMEM((blocks + 2, blocks, size, size), bf16),
-            pltpu.VMEM((blocks, size, head_size), f32),
-            pltpu.VMEM((blocks, size, head_size), f32),
+            pltpu.VMEM((blocks + 2, size, head_size), f32),
+            pltpu.VMEM((blocks + 2, size, head_size), f32),
+            pltpu.VMEM((blocks + 2, head_size, size), f32),
+            pltpu.VMEM((blocks + 2, 1, size), f32),
             pltpu.SemaphoreType.DMA((4, 2, shards)),
             pltpu.SemaphoreType.DMA((4, 3 * shards)),
             pltpu.SemaphoreType.DMA((4, 2 * shards)),

time: 74.9 us -> 76 us (1.015)
  Pallas kernels: 73.9 us -> 75 us
    pallas_call x1, Pallas kernels: 70.8 us -> 72 us  [by_heads(): pl.pallas_call(functools.partial(head_kernel, shards, half, group), out_s...]
where the time goes in v5:
time: 76 us; the launch traced here: 75.8 us
  Pallas kernels  75 us (99%)
  between operations  0.82 us (1%)
    pallas_call x1, Pallas kernels, by_heads(): pl.pallas_call(functools.partial(head_kernel, shards, half, group), out_s...  72 us
    pallas_call x1, Pallas kernels, by_heads(): pl.pallas_call(rows_kernel, out_shape=[rows_first] * 4, in_specs=[pl.Bloc...  3.05 us

profile of v5, /device:TPU:0, one launch (start us, length us, event | category | flops | bytes accessed | tf_op | source)
XLA Modules:
  0.0 75.8 jit_solution(9137483845107980900)
XLA Ops:
  0.6 72.0 %shard_map.84 = (bf16[4,8,192,128]{3,2,1,0:T(8,128)(2,1)}, bf16[2,6,96,128]{3,2,1,0:T(8,128)(2,1)}) custom-call(bf16[192,8,128]{2,1,0:T(8,128)(2,1)} %key_ref.1, bf16[192,8,128]{2,1,0:T(8,128)(2,1)} %query_ref.1, bf16[192,8,128]{2,1,0:T(8,128)(2,1)} %value_ref.1, bf16[192,8,128]{2,1,0:T(8,128)(2,1)} %grad_ref.1, s32[1536]{0:T(1024)} %doc_ref.1), custom_call_target="tpu_custom_call" | custom-call | flops 2113929216 | bytes 3145728 | tf_op jit(solution)/shard_map/pallas_call | solution.py:716
  72.6 3.0 %shard_map.85 = (bf16[192,8,128]{2,1,0:T(8,128)(2,1)}, bf16[192,8,128]{2,1,0:T(8,128)(2,1)}, bf16[192,8,128]{2,1,0:T(8,128)(2,1)}, bf16[192,8,128]{2,1,0:T(8,128)(2,1)}) custom-call(bf16[4,8,192,128]{3,2,1,0:T(8,128)(2,1)} %get-tuple-element.6.heads_ref, bf16[2,6,96,128]{3,2,1,0:T(8,128)(2,1)} %get-tuple-element.7.more_ref), custom_call_target="tpu_custom_call" | custom-call | bytes 3145728 | tf_op jit(solution)/shard_map/pallas_call | solution.py:760

commit v6 on v5

--- a/solution.py
+++ b/solution.py
@@ -378,6 +378,7 @@
     for kind in (KEY, QUERY, VALUE):
         send_low(kind)
     stage(GRAD)
+    send_low(GRAD)
 
     docs = doc_ref[...].astype(jnp.float32).reshape(1, -1)
     for block in range(blocks):
@@ -514,57 +515,49 @@
     for kind, part in ((KEY, 1), (QUERY, 0)):
         sent_in(kind, 1)
         send_in(GRAD, part)
-    send_low(GRAD)
-    pl.when(low)(lambda: forward(blocks, me + lower))
-    pl.when(helping)(lambda: forward(blocks + 1, me - lower))
-    for block in range(2, blocks):
-        forward(block)
-
-    def lower_backward():
-        late = blocks - 1
-        first = [(late, 2), (2, 2), (2, 1), (2, 0), (late, 1)]
-        backward(first, plan(first), [("k", 2, 2), ("q", 2, 0)])
-
-        def second():
-            ready_grads(1)
-            backward(
-                [(1, 1), (1, 0)], [("q", 1, 1)], [("k", 1, 1), ("q", 1, 0)]
-            )
-
-        either(helped, lambda: finish_keys(1, value_acc[1], key_acc[1]), second)
-        home = [(late, 0), (late, late)]
-        backward(home, [("k", late, late)], [("k", late, late), ("q", late, late)])
-        ready_grads(0)
-        backward([(0, 0)], [("q", 0, 0)], [("k", 0, 0), ("q", 0, 0)])
+
+    @pl.when(low)
+    def _():
         extra = blocks
+        forward(extra, me + lower)
         ready_grads(extra)
         both = [("q", extra, extra), ("k", extra, extra)]
         backward([(extra, extra)], both, both, me + lower)
 
+    @pl.when(helping)
+    def _():
+        extra = blocks + 1
+        forward(extra, me - lower)
+        ready_grads(extra)
+        pairs = [(extra, blocks), (extra, extra)]
+        done = [("k", extra, blocks), ("k", extra, extra), ("q", extra, extra)]
+        backward(pairs, plan(pairs), done, me - lower)
+
+    for block in range(2, blocks):
+        forward(block)
+
+    def lower_backward():
+        late = blocks - 1
+        first = [(late, late), (late, 2), (2, 2), (2, 1), (2, 0), (late, 1), (late, 0)]
+        done = [("k", late, late), ("k", 2, 2), ("q", 2, 0), ("q", late, 0)]
+        backward(first, plan(first), done)
+
+        def second():
+            ready_grads(1)
+            backward([(1, 1), (1, 0)], [("q", 1, 1)], [("k", 1, 1), ("q", 1, 0)])
+
+        either(helped, lambda: finish_keys(1, value_acc[1], key_acc[1]), second)
+        ready_grads(0)
+        backward([(0, 0)], [("q", 0, 0)], [("k", 0, 0), ("q", 0, 0)])
+
     def upper_backward():
         late = blocks - 1
-        first = [(late, late), (late, 2), (late, 1), (late, 0), (2, 0)]
-        backward(first, plan(first), [("k", late, late), ("q", late, 0)])
+        first = [(late, late), (late, 2), (2, 2), (late, 1), (late, 0), (2, 1), (2, 0)]
+        done = [("k", late, late), ("k", 2, 2), ("q", late, 0), ("q", 2, 0)]
+        backward(first, plan(first), done)
         ready_grads(1)
-        backward([(1, 0)], [("q", 1, 0)], [("k", 1, 0)])
-
-        @pl.when(helping)
-        def _():
-            extra = blocks + 1
-            ready_grads(extra)
-            pairs = [(extra, blocks), (extra, extra)]
-            backward(
-                pairs,
-                plan(pairs),
-                [("k", extra, blocks), ("k", extra, extra), ("q", extra, extra)],
-                me - lower,
-            )
-
-        backward(
-            [(2, 2), (2, 1), (1, 1)],
-            [],
-            [("k", 2, 2), ("q", 2, 1), ("k", 1, 1), ("q", 1, 1)],
-        )
+        done = [("k", 1, 0), ("k", 1, 1), ("q", 1, 1)]
+        backward([(1, 0), (1, 1)], [("q", 1, 0)], done)
         pltpu.make_async_copy(zeros, spare, zero_sem).wait()
 
     for block in range(2, blocks):

time: 76 us -> 73.4 us (0.966)
  Pallas kernels: 75 us -> 72.4 us
    pallas_call x1, Pallas kernels: 72 us -> 69.4 us  [by_heads(): pl.pallas_call(functools.partial(head_kernel, shards, half, group), out_s...]
where the time goes in v6:
time: 73.4 us; the launch traced here: 73.2 us
  Pallas kernels  72.4 us (99%)
  between operations  0.8 us (1%)
    pallas_call x1, Pallas kernels, by_heads(): pl.pallas_call(functools.partial(head_kernel, shards, half, group), out_s...  69.4 us
    pallas_call x1, Pallas kernels, by_heads(): pl.pallas_call(rows_kernel, out_shape=[rows_first] * 4, in_specs=[pl.Bloc...  3.05 us

profile of v6, /device:TPU:0, one launch (start us, length us, event | category | flops | bytes accessed | tf_op | source)
XLA Modules:
  0.0 73.2 jit_solution(5927530862216932887)
XLA Ops:
  0.6 69.4 %shard_map.84 = (bf16[4,8,192,128]{3,2,1,0:T(8,128)(2,1)}, bf16[2,6,96,128]{3,2,1,0:T(8,128)(2,1)}) custom-call(bf16[192,8,128]{2,1,0:T(8,128)(2,1)} %key_ref.1, bf16[192,8,128]{2,1,0:T(8,128)(2,1)} %query_ref.1, bf16[192,8,128]{2,1,0:T(8,128)(2,1)} %value_ref.1, bf16[192,8,128]{2,1,0:T(8,128)(2,1)} %grad_ref.1, s32[1536]{0:T(1024)} %doc_ref.1), custom_call_target="tpu_custom_call" | custom-call | flops 2113929216 | bytes 3145728 | tf_op jit(solution)/shard_map/pallas_call | solution.py:709
  70.0 3.0 %shard_map.85 = (bf16[192,8,128]{2,1,0:T(8,128)(2,1)}, bf16[192,8,128]{2,1,0:T(8,128)(2,1)}, bf16[192,8,128]{2,1,0:T(8,128)(2,1)}, bf16[192,8,128]{2,1,0:T(8,128)(2,1)}) custom-call(bf16[4,8,192,128]{3,2,1,0:T(8,128)(2,1)} %get-tuple-element.6.heads_ref, bf16[2,6,96,128]{3,2,1,0:T(8,128)(2,1)} %get-tuple-element.7.more_ref), custom_call_target="tpu_custom_call" | custom-call | bytes 3145728 | tf_op jit(solution)/shard_map/pallas_call | solution.py:753

commit v7 on v6

--- a/solution.py
+++ b/solution.py
@@ -510,11 +510,12 @@
         pltpu.make_async_copy(zeros, spare, zero_sem).start()
         keys_alone(0)
 
-    either(low, lambda: forward(0), fill_zeros)
-    either(helped, lambda: keys_alone(1), lambda: forward(1))
     for kind, part in ((KEY, 1), (QUERY, 0)):
         sent_in(kind, 1)
         send_in(GRAD, part)
+
+    either(low, lambda: forward(0), fill_zeros)
+    either(helped, lambda: keys_alone(1), lambda: forward(1))
 
     @pl.when(low)
     def _():

time: 73.4 us -> 73.4 us (level)
  no operation moved by 1% of the time
where the time goes in v7:
time: 73.4 us; the launch traced here: 73.2 us
  Pallas kernels  72.4 us (99%)
  between operations  0.8 us (1%)
    pallas_call x1, Pallas kernels, by_heads(): pl.pallas_call(functools.partial(head_kernel, shards, half, group), out_s...  69.3 us
    pallas_call x1, Pallas kernels, by_heads(): pl.pallas_call(rows_kernel, out_shape=[rows_first] * 4, in_specs=[pl.Bloc...  3.05 us

profile of v7, /device:TPU:0, one launch (start us, length us, event | category | flops | bytes accessed | tf_op | source)
XLA Modules:
  0.0 73.2 jit_solution(16016080293660181875)
XLA Ops:
  0.6 69.3 %shard_map.84 = (bf16[4,8,192,128]{3,2,1,0:T(8,128)(2,1)}, bf16[2,6,96,128]{3,2,1,0:T(8,128)(2,1)}) custom-call(bf16[192,8,128]{2,1,0:T(8,128)(2,1)} %key_ref.1, bf16[192,8,128]{2,1,0:T(8,128)(2,1)} %query_ref.1, bf16[192,8,128]{2,1,0:T(8,128)(2,1)} %value_ref.1, bf16[192,8,128]{2,1,0:T(8,128)(2,1)} %grad_ref.1, s32[1536]{0:T(1024)} %doc_ref.1), custom_call_target="tpu_custom_call" | custom-call | flops 2113929216 | bytes 3145728 | tf_op jit(solution)/shard_map/pallas_call | solution.py:710
  70.0 3.0 %shard_map.85 = (bf16[192,8,128]{2,1,0:T(8,128)(2,1)}, bf16[192,8,128]{2,1,0:T(8,128)(2,1)}, bf16[192,8,128]{2,1,0:T(8,128)(2,1)}, bf16[192,8,128]{2,1,0:T(8,128)(2,1)}) custom-call(bf16[4,8,192,128]{3,2,1,0:T(8,128)(2,1)} %get-tuple-element.6.heads_ref, bf16[2,6,96,128]{3,2,1,0:T(8,128)(2,1)} %get-tuple-element.7.more_ref), custom_call_target="tpu_custom_call" | custom-call | bytes 3145728 | tf_op jit(solution)/shard_map/pallas_call | solution.py:754
